TPU v7x, 256 devices: a whole 4x4x8 slice. The times are simulated.
256 devices in a mesh: dp: 4 (over y_hi, core), ctx: 64 (over y_lo, x, z).
Axes of the slice: x: 4, y: 4 (y_hi: 2, y_lo: 2; y = y_hi * 2 + y_lo), z: 8, core: 2. Of those that a mesh axis runs over, the one named last changes fastest.
Arguments:
- inputs: bfloat16 [4, 8192, 512], P('dp', 'ctx'), may hold values from -6 to 6
- grad_out: bfloat16 [4, 8192, 512], P('dp', 'ctx'), may hold values from -6 to 6
- log_dt: float32 [512], replicated, as said below
- log_a_re: float32 [512, 64], replicated, may hold values from -1.5 to 0.5
- a_im: float32 [512, 64], replicated, may hold values from -100 to 100
- c_re: float32 [512, 64], replicated, may hold values from -6 to 6
- c_im: float32 [512, 64], replicated, may hold values from -6 to 6
- skip_gain: float32 [512], replicated, may hold values from -6 to 6
Outputs:
- grad_inputs: bfloat16 [4, 8192, 512], P('dp', 'ctx')
- grad_log_dt: float32 [512], replicated
- grad_log_a_re: float32 [512, 64], replicated
- grad_a_im: float32 [512, 64], replicated
- grad_c_re: float32 [512, 64], replicated
- grad_c_im: float32 [512, 64], replicated
- grad_skip: float32 [512], replicated
Inputs may be any that keep to these rules, and one draw needn't show every extreme that they name: exp(log_dt) is positive and below one.
All inputs are finite; a program needn't handle non-finite values.
Results may differ from a plain program's by a relative error of at most 0.013.
Values may be sent and summed in bfloat16 or wider, within the bound.
No kernel may reach another device: no remote copies, remote signals or barrier semaphores. Data moves between devices by JAX's collectives and lax.ppermute only.
A program may use at most 64 MiB of HBM per device.

v0:
```python
import math

import jax
import jax.numpy as jnp
from jax import lax
from jax.sharding import PartitionSpec as P

HIGHEST = lax.Precision.HIGHEST
TWO_PI = 2.0 * math.pi


def shortened(value):
    return jax.tree.map(lambda a: a.astype(jnp.bfloat16) if a.dtype == jnp.float32 else a, value)


def pole_terms(log_dt, log_a_re, a_im, c_re, c_im):
    step_size = jnp.exp(log_dt)[:, None]
    pole_re = -jnp.exp(log_a_re)
    w_re = step_size * pole_re
    w_im = step_size * a_im
    growth = jnp.exp(w_re)
    half_sin = jnp.sin(0.5 * w_im)
    e_re = jnp.expm1(w_re) * jnp.cos(w_im) - 2.0 * half_sin * half_sin
    e_im = growth * jnp.sin(w_im)
    n_re = e_re * c_re - e_im * c_im
    n_im = e_re * c_im + e_im * c_re
    modulus = pole_re * pole_re + a_im * a_im
    ct_re = (n_re * pole_re + n_im * a_im) / modulus
    ct_im = (n_im * pole_re - n_re * a_im) / modulus
    return (w_re, w_im, ct_re, ct_im)


def kernel_block(log_dt, log_a_re, a_im, c_re, c_im, positions):
    w_re, w_im, ct_re, ct_im = pole_terms(log_dt, log_a_re, a_im, c_re, c_im)
    phase = w_im[:, :, None] * positions
    decays = jnp.exp(w_re[:, :, None] * positions)
    wave_re = decays * jnp.cos(phase)
    wave_im = decays * jnp.sin(phase)
    return 2.0 * jnp.sum(ct_re[:, :, None] * wave_re - ct_im[:, :, None] * wave_im, axis=1)


def twiddles(rows_idx, cols_idx, modulus):
    product = rows_idx[:, None] * cols_idx[None, :] % modulus
    angles = product.astype(jnp.float32) * (TWO_PI / modulus)
    return (jnp.cos(angles), jnp.sin(angles))


def block_width():
    return 64


def kernel_rows(params, positions):
    channels = params[0].shape[0]
    width_blk = block_width()
    nblocks = channels // width_blk
    grouped = tuple((source.reshape((nblocks, width_blk) + source.shape[1:]) for source in params))

    def one_block(operands):
        return kernel_block(
            operands[0], operands[1], operands[2], operands[3], operands[4], positions
        )

    rows_out = lax.map(one_block, grouped)
    return rows_out.reshape(channels, positions.shape[0]).T


def kernel_pullback(params, positions, cotangent):
    channels = params[0].shape[0]
    width_blk = block_width()
    nblocks = channels // width_blk
    grouped = tuple((source.reshape((nblocks, width_blk) + source.shape[1:]) for source in params))
    cot_blocks = cotangent.reshape(nblocks, width_blk, cotangent.shape[1])

    def one_block(operands):

        def local_kernel(arg_one, arg_two, arg_three, arg_four, arg_five):
            return kernel_block(arg_one, arg_two, arg_three, arg_four, arg_five, positions)

        unused, pull = jax.vjp(
            local_kernel, operands[0], operands[1], operands[2], operands[3], operands[4]
        )
        return pull(operands[5])

    pulled = lax.map(one_block, grouped + (cot_blocks,))
    return tuple((item.reshape((channels,) + item.shape[2:]) for item in pulled))


def spectrum(blocks, place, devices):
    span_len = blocks.shape[2]
    tokens = span_len * devices
    wide_len = 2 * devices
    points = wide_len * tokens
    freq_one = jnp.arange(wide_len, dtype=jnp.int32)
    block_idx = jnp.arange(devices, dtype=jnp.int32)
    cos_one, sin_one = twiddles(freq_one, block_idx, wide_len)
    real_part = jnp.einsum("kp,spjh->skjh", cos_one, blocks, precision=HIGHEST)
    imag_part = -jnp.einsum("kp,spjh->skjh", sin_one, blocks, precision=HIGHEST)
    local_pos = place * span_len + jnp.arange(span_len, dtype=jnp.int32)
    cos_turn, sin_turn = twiddles(freq_one, local_pos, points)
    cos_turn = cos_turn[None, :, :, None]
    sin_turn = sin_turn[None, :, :, None]
    twisted_re = real_part * cos_turn + imag_part * sin_turn
    twisted_im = imag_part * cos_turn - real_part * sin_turn
    rows_re, rows_im = (
        lax.all_to_all(twisted_re, "ctx", split_axis=1, concat_axis=2, tiled=True),
        lax.all_to_all(twisted_im, "ctx", split_axis=1, concat_axis=2, tiled=True),
    )
    freq_two = jnp.arange(tokens, dtype=jnp.int32)
    cos_two, sin_two = twiddles(freq_two, freq_two, tokens)
    out_re = jnp.einsum("kn,sanh->sakh", cos_two, rows_re, precision=HIGHEST) + jnp.einsum(
        "kn,sanh->sakh", sin_two, rows_im, precision=HIGHEST
    )
    out_im = jnp.einsum("kn,sanh->sakh", cos_two, rows_im, precision=HIGHEST) - jnp.einsum(
        "kn,sanh->sakh", sin_two, rows_re, precision=HIGHEST
    )
    return (out_re, out_im)


def signal(spec_re, spec_im, place, devices):
    tokens = spec_re.shape[2]
    span_len = tokens // devices
    wide_len = 2 * devices
    points = wide_len * tokens
    freq_two = jnp.arange(tokens, dtype=jnp.int32)
    cos_two, sin_two = twiddles(freq_two, freq_two, tokens)
    rows_re = jnp.einsum("nk,sakh->sanh", cos_two, spec_re, precision=HIGHEST) - jnp.einsum(
        "nk,sakh->sanh", sin_two, spec_im, precision=HIGHEST
    )
    rows_im = jnp.einsum("nk,sakh->sanh", cos_two, spec_im, precision=HIGHEST) + jnp.einsum(
        "nk,sakh->sanh", sin_two, spec_re, precision=HIGHEST
    )
    cols_re, cols_im = (
        lax.all_to_all(shortened(rows_re), "ctx", split_axis=2, concat_axis=1, tiled=True).astype(
            rows_re.dtype
        ),
        lax.all_to_all(shortened(rows_im), "ctx", split_axis=2, concat_axis=1, tiled=True).astype(
            rows_im.dtype
        ),
    )
    freq_one = jnp.arange(wide_len, dtype=jnp.int32)
    local_pos = place * span_len + jnp.arange(span_len, dtype=jnp.int32)
    cos_turn, sin_turn = twiddles(freq_one, local_pos, points)
    cos_turn = cos_turn[None, :, :, None]
    sin_turn = sin_turn[None, :, :, None]
    turned_re = cols_re * cos_turn - cols_im * sin_turn
    turned_im = cols_im * cos_turn + cols_re * sin_turn
    block_idx = jnp.arange(devices, dtype=jnp.int32)
    cos_one, sin_one = twiddles(block_idx, freq_one, wide_len)
    values = jnp.einsum("pk,skjh->spjh", cos_one, turned_re, precision=HIGHEST) - jnp.einsum(
        "pk,skjh->spjh", sin_one, turned_im, precision=HIGHEST
    )
    values = values * (1.0 / points)
    placed = lax.all_to_all(
        shortened(values), "ctx", split_axis=1, concat_axis=2, tiled=True
    ).astype(values.dtype)
    return placed.reshape(tokens, placed.shape[3])


def body(inputs, grad_out, log_dt, log_a_re, a_im, c_re, c_im, skip_gain):
    devices = lax.axis_size("ctx")
    place = lax.axis_index("ctx")
    tokens = inputs.shape[1]
    channels = inputs.shape[2]
    positions = (place * tokens + jnp.arange(tokens, dtype=jnp.int32)).astype(jnp.float32)
    params = (log_dt, log_a_re, a_im, c_re, c_im)
    input_cols, output_cols = (
        lax.all_to_all(inputs, "ctx", split_axis=1, concat_axis=0, tiled=True),
        lax.all_to_all(grad_out, "ctx", split_axis=1, concat_axis=0, tiled=True),
    )
    kernel = kernel_rows(params, positions)
    kernel_cols = lax.all_to_all(
        kernel[None].astype(jnp.bfloat16), "ctx", split_axis=1, concat_axis=0, tiled=True
    ).astype(jnp.float32)
    stacked = jnp.stack(
        [input_cols.astype(jnp.float32), output_cols.astype(jnp.float32), kernel_cols]
    )
    spec_re, spec_im = spectrum(stacked, place, devices)
    ker_re, ker_im = (spec_re[2], spec_im[2])
    in_re, out_re = (spec_re[0], spec_re[1])
    in_im, out_im = (spec_im[0], spec_im[1])
    lag_re = out_re * in_re + out_im * in_im
    lag_im = out_im * in_re - out_re * in_im
    back_re = out_re * ker_re + out_im * ker_im
    back_im = out_im * ker_re - out_re * ker_im
    both_re = jnp.concatenate([back_re, lag_re], axis=2)[None]
    both_im = jnp.concatenate([back_im, lag_im], axis=2)[None]
    values = signal(both_re, both_im, place, devices)
    grad_rows = values[:, :channels] + skip_gain * grad_out[0].astype(jnp.float32)
    grad_inputs = grad_rows.astype(jnp.bfloat16)[None]
    lag_vals = values[:, channels:]
    pulled = kernel_pullback(params, positions, lag_vals.T)
    skip_part = jnp.sum(inputs[0].astype(jnp.float32) * grad_out[0].astype(jnp.float32), axis=0)
    totals = lax.psum(
        (pulled[0], pulled[1], pulled[2], pulled[3], pulled[4], skip_part), ("dp", "ctx")
    )
    return (grad_inputs, totals[0], totals[1], totals[2], totals[3], totals[4], totals[5])


def solution(mesh):
    placed = (P("dp", "ctx", None), P("dp", "ctx", None), P(), P(), P(), P(), P(), P())
    return jax.shard_map(
        body,
        mesh=mesh,
        in_specs=placed,
        out_specs=(P("dp", "ctx", None), P(), P(), P(), P(), P(), P()),
        check_vma=False,
    )
```

profile of v0, /device:TPU:1, one launch (start us, length us, event | category | flops | bytes accessed | tf_op | source)
XLA Modules:
  0.0 704.1 jit_solution(17461364914382083473)
XLA Ops:
  11.4 73.6 %while.30 = (s32[]{:T(128)}, bf16[8,64,128]{2,1,0:T(8,128)(2,1)S(1)}, f32[8,64]{1,0:T(8,128)S(1)}, f32[8,64,64]{2,1,0:T(8,128)S(1)}, f32[8,64,64]{2,1,0:T(8,128)...) while((s32[]{:T(128)}, ...), condition=%wide.region_2.3_spmd.clone, body=%wide.region_0.2_spmd.clone.sunk | while | flops 4317442 | bytes 395121 | solution.py:63
  11.8 8.7 %fusion.235 = f32[64,128]{1,0:T(8,128)S(1)} fusion(f32[64,64]{1,0:T(8,128)S(1)} %fusion.234, f32[64,64]{1,0:T(8,128)S(1)} %get-tuple-element.419, f32[128]{0:T(128)S(1)} %add_convert_fusion.4, f32[64,64]{1,0:T(8,128)S(1)} %get-tuple-element.420, f32[64,64]{1,0:T(8,128)S(1)} %get-tuple-element.421), kind=kLoop, calls=%fused_computation.7.clone.1 | loop fusion | flops 4186112 | bytes 98816 | tf_op jit(solution)/shard_map/while/body/eval_jaxpr/reduce_sum | solution.py:39
  21.0 8.7 %fusion.235 = f32[64,128]{1,0:T(8,128)S(1)} fusion(f32[64,64]{1,0:T(8,128)S(1)} %fusion.234, f32[64,64]{1,0:T(8,128)S(1)} %get-tuple-element.419, f32[128]{0:T(128)S(1)} %add_convert_fusion.4, f32[64,64]{1,0:T(8,128)S(1)} %get-tuple-element.420, f32[64,64]{1,0:T(8,128)S(1)} %get-tuple-element.421), kind=kLoop, calls=%fused_computation.7.clone.1 | loop fusion | flops 4186112 | bytes 98816 | tf_op jit(solution)/shard_map/while/body/eval_jaxpr/reduce_sum | solution.py:39
  30.2 8.7 %fusion.235 = f32[64,128]{1,0:T(8,128)S(1)} fusion(f32[64,64]{1,0:T(8,128)S(1)} %fusion.234, f32[64,64]{1,0:T(8,128)S(1)} %get-tuple-element.419, f32[128]{0:T(128)S(1)} %add_convert_fusion.4, f32[64,64]{1,0:T(8,128)S(1)} %get-tuple-element.420, f32[64,64]{1,0:T(8,128)S(1)} %get-tuple-element.421), kind=kLoop, calls=%fused_computation.7.clone.1 | loop fusion | flops 4186112 | bytes 98816 | tf_op jit(solution)/shard_map/while/body/eval_jaxpr/reduce_sum | solution.py:39
  39.4 8.7 %fusion.235 = f32[64,128]{1,0:T(8,128)S(1)} fusion(f32[64,64]{1,0:T(8,128)S(1)} %fusion.234, f32[64,64]{1,0:T(8,128)S(1)} %get-tuple-element.419, f32[128]{0:T(128)S(1)} %add_convert_fusion.4, f32[64,64]{1,0:T(8,128)S(1)} %get-tuple-element.420, f32[64,64]{1,0:T(8,128)S(1)} %get-tuple-element.421), kind=kLoop, calls=%fused_computation.7.clone.1 | loop fusion | flops 4186112 | bytes 98816 | tf_op jit(solution)/shard_map/while/body/eval_jaxpr/reduce_sum | solution.py:39
  48.6 8.7 %fusion.235 = f32[64,128]{1,0:T(8,128)S(1)} fusion(f32[64,64]{1,0:T(8,128)S(1)} %fusion.234, f32[64,64]{1,0:T(8,128)S(1)} %get-tuple-element.419, f32[128]{0:T(128)S(1)} %add_convert_fusion.4, f32[64,64]{1,0:T(8,128)S(1)} %get-tuple-element.420, f32[64,64]{1,0:T(8,128)S(1)} %get-tuple-element.421), kind=kLoop, calls=%fused_computation.7.clone.1 | loop fusion | flops 4186112 | bytes 98816 | tf_op jit(solution)/shard_map/while/body/eval_jaxpr/reduce_sum | solution.py:39
  57.8 8.7 %fusion.235 = f32[64,128]{1,0:T(8,128)S(1)} fusion(f32[64,64]{1,0:T(8,128)S(1)} %fusion.234, f32[64,64]{1,0:T(8,128)S(1)} %get-tuple-element.419, f32[128]{0:T(128)S(1)} %add_convert_fusion.4, f32[64,64]{1,0:T(8,128)S(1)} %get-tuple-element.420, f32[64,64]{1,0:T(8,128)S(1)} %get-tuple-element.421), kind=kLoop, calls=%fused_computation.7.clone.1 | loop fusion | flops 4186112 | bytes 98816 | tf_op jit(solution)/shard_map/while/body/eval_jaxpr/reduce_sum | solution.py:39
  67.0 8.7 %fusion.235 = f32[64,128]{1,0:T(8,128)S(1)} fusion(f32[64,64]{1,0:T(8,128)S(1)} %fusion.234, f32[64,64]{1,0:T(8,128)S(1)} %get-tuple-element.419, f32[128]{0:T(128)S(1)} %add_convert_fusion.4, f32[64,64]{1,0:T(8,128)S(1)} %get-tuple-element.420, f32[64,64]{1,0:T(8,128)S(1)} %get-tuple-element.421), kind=kLoop, calls=%fused_computation.7.clone.1 | loop fusion | flops 4186112 | bytes 98816 | tf_op jit(solution)/shard_map/while/body/eval_jaxpr/reduce_sum | solution.py:39
  76.2 8.7 %fusion.235 = f32[64,128]{1,0:T(8,128)S(1)} fusion(f32[64,64]{1,0:T(8,128)S(1)} %fusion.234, f32[64,64]{1,0:T(8,128)S(1)} %get-tuple-element.419, f32[128]{0:T(128)S(1)} %add_convert_fusion.4, f32[64,64]{1,0:T(8,128)S(1)} %get-tuple-element.420, f32[64,64]{1,0:T(8,128)S(1)} %get-tuple-element.421), kind=kLoop, calls=%fused_computation.7.clone.1 | loop fusion | flops 4186112 | bytes 98816 | tf_op jit(solution)/shard_map/while/body/eval_jaxpr/reduce_sum | solution.py:39
  87.9 13.5 %all-to-all-start.2 = ((bf16[64,2,512]{2,1,0:T(2,128)(2,1)}), bf16[64,2,512]{2,1,0:T(2,128)(2,1)S(1)}, u32[]{:S(2)}, u32[]{:S(2)}) async-start(bf16[64,2,512]{2,1,0:T(2,128)(2,1)} %reshape.721), calls=%async_computation.2 | async-start | bytes 262144 | tf_op jit(solution)/shard_map/all_to_all | solution.py:171
  106.1 5.3 all-to-all-done.2
  111.4 5.5 all-to-all-start
  117.8 9.0 %all-to-all-done = bf16[64,2,512]{2,1,0:T(2,128)(2,1)S(1)} async-done(((bf16[64,2,512]{2,1,0:T(2,128)(2,1)}), bf16[64,2,512]{2,1,0:T(2,128)(2,1)S(1)}, u32[]{:S(2)}, u32[]{:S(2)}) %all-to-all-start) | async-done | bytes 131104 | tf_op jit(solution)/shard_map/all_to_all | solution.py:167
  126.8 5.1 all-to-all-start.1
  133.0 9.0 %all-to-all-done.1 = bf16[64,2,512]{2,1,0:T(2,128)(2,1)S(1)} async-done(((bf16[64,2,512]{2,1,0:T(2,128)(2,1)}), bf16[64,2,512]{2,1,0:T(2,128)(2,1)S(1)}, u32[]{:S(2)}, u32[]{:S(2)}) %all-to-all-start.1) | async-done | bytes 131104 | tf_op jit(solution)/shard_map/all_to_all | solution.py:168
  144.0 2.2 fusion.78
  146.2 2.2 copy.162
  148.4 4.7 all-to-all-start.3
  153.1 2.2 copy.166
  155.2 32.6 %all-to-all-done.3 = f32[3,128,2,512]{3,2,0,1:T(2,128)S(1)} async-done(((f32[3,128,2,512]{3,2,0,1:T(2,128)}), f32[3,128,2,512]{3,2,0,1:T(2,128)S(1)}, u32[]{:S(2)}, u32[]{:S(2)}) %all-to-all-start.3) | async-done | bytes 1572896 | tf_op jit(solution)/shard_map/all_to_all | solution.py:105
  187.9 8.2 %all-to-all-start.4 = ((f32[3,128,2,512]{3,2,0,1:T(2,128)}), f32[3,128,2,512]{3,2,0,1:T(2,128)S(1)}, u32[]{:S(2)}, u32[]{:S(2)}) async-start(f32[3,128,2,512]{3,2,0,1:T(2,128)} %copy.166), calls=%async_computation.4 | async-start | bytes 3145728 | tf_op jit(solution)/shard_map/all_to_all | solution.py:106
  196.1 2.0 copy.164
  198.1 2.5 copy.165
  200.6 2.8 fusion.109
  203.3 27.1 %all-to-all-done.4 = f32[3,128,2,512]{3,2,0,1:T(2,128)S(1)} async-done(((f32[3,128,2,512]{3,2,0,1:T(2,128)}), f32[3,128,2,512]{3,2,0,1:T(2,128)S(1)}, u32[]{:S(2)}, u32[]{:S(2)}) %all-to-all-start.4) | async-done | bytes 1572896 | tf_op jit(solution)/shard_map/all_to_all | solution.py:106
  230.4 2.0 copy.168
  232.4 2.5 copy.169
  234.9 1.7 fusion.107
  236.6 1.7 add_bitcast_fusion
  238.3 1.7 subtract_bitcast_fusion
  243.9 8.1 %all-to-all-start.5 = ((bf16[1,2,128,1024]{3,1,0,2:T(2,128)(2,1)}), bf16[1,2,128,1024]{3,1,0,2:T(2,128)(2,1)S(1)}, u32[]{:S(2)}, u32[]{:S(2)}) async-start(bf16[1,2,128,1024]{3,1,0,2:T(2,128)(2,1)} %copy.172), calls=%async_computation.5 | async-start | bytes 1048576 | tf_op jit(solution)/shard_map/all_to_all | solution.py:133
  255.6 9.8 %all-to-all-done.5 = bf16[1,2,128,1024]{3,1,0,2:T(2,128)(2,1)S(1)} async-done(((bf16[1,2,128,1024]{3,1,0,2:T(2,128)(2,1)}), bf16[1,2,128,1024]{3,1,0,2:T(2,128)(2,1)S(1)}, u32[]{:S(2)}, u32[]{:S(2)}) %all-to-all-start.5) | async-done | bytes 524320 | tf_op jit(solution)/shard_map/all_to_all | solution.py:133
  265.4 5.2 all-to-all-start.6
  271.9 12.0 %all-to-all-done.6 = bf16[1,2,128,1024]{3,1,0,2:T(2,128)(2,1)S(1)} async-done(((bf16[1,2,128,1024]{3,1,0,2:T(2,128)(2,1)}), bf16[1,2,128,1024]{3,1,0,2:T(2,128)(2,1)S(1)}, u32[]{:S(2)}, u32[]{:S(2)}) %all-to-all-start.6) | async-done | bytes 524320 | tf_op jit(solution)/shard_map/all_to_all | solution.py:136
  289.4 5.1 all-to-all-start.7
  294.9 10.6 %all-to-all-done.7 = bf16[1,64,2,1024]{3,2,0,1:T(2,128)(2,1)S(1)} async-done(((bf16[1,64,2,1024]{3,2,0,1:T(2,128)(2,1)}), bf16[1,64,2,1024]{3,2,0,1:T(2,128)(2,1)S(1)}, u32[]{:S(2)}, u32[]{:S(2)}) %all-to-all-start.7) | async-done | bytes 262176 | tf_op jit(solution)/shard_map/all_to_all | solution.py:153
  306.5 125.9 %while.31 = (s32[]{:T(128)}, f32[8,64]{1,0:T(8,128)S(1)}, f32[8,64,64]{2,1,0:T(8,128)S(1)}, f32[8,64,64]{2,1,0:T(8,128)S(1)}, f32[8,64,64]{2,1,0:T(8,128)S(1)}, ...) while((s32[]{:T(128)}, f32[8,64]{1,0:T(8,128)S(1)}, ...), condition=%wide.region_10.11_spmd.clone, body=%wide.region_3.10_spmd.clone.sunk | while | flops 13332738 | bytes 1594553 | solution.py:84
  307.9 11.7 %fusion.241 = (f32[64,64]{1,0:T(8,128)S(1)}, f32[64,64]{1,0:T(8,128)S(1)}, f32[64,64]{1,0:T(8,128)S(1)}, f32[64,64]{1,0:T(8,128)S(1)}) fusion(f32[64,128]{1,0:T(8,128)S(1)} %get-tuple-element.436, f32[64,64]{1,0:T(8,128)S(1)} %fusion.240, f32[64,64]{1,0:T(8,128)S(1)} %get-tuple-element.435, f32[64,128]{1,0:T(8,128)S(1)} %get-tuple-element.440, ...), kind=kLoop, calls=%fused_computation.55.clone.1 | loop fusion | flops 12566528 | bytes 197120 | tf_op jit(solution)/shard_map/while/body/eval_jaxpr/transpose(jvp())/reduce_sum | solution.py:36
  323.6 11.7 %fusion.241 = (f32[64,64]{1,0:T(8,128)S(1)}, f32[64,64]{1,0:T(8,128)S(1)}, f32[64,64]{1,0:T(8,128)S(1)}, f32[64,64]{1,0:T(8,128)S(1)}) fusion(f32[64,128]{1,0:T(8,128)S(1)} %get-tuple-element.436, f32[64,64]{1,0:T(8,128)S(1)} %fusion.240, f32[64,64]{1,0:T(8,128)S(1)} %get-tuple-element.435, f32[64,128]{1,0:T(8,128)S(1)} %get-tuple-element.440, ...), kind=kLoop, calls=%fused_computation.55.clone.1 | loop fusion | flops 12566528 | bytes 197120 | tf_op jit(solution)/shard_map/while/body/eval_jaxpr/transpose(jvp())/reduce_sum | solution.py:36
  339.4 11.7 %fusion.241 = (f32[64,64]{1,0:T(8,128)S(1)}, f32[64,64]{1,0:T(8,128)S(1)}, f32[64,64]{1,0:T(8,128)S(1)}, f32[64,64]{1,0:T(8,128)S(1)}) fusion(f32[64,128]{1,0:T(8,128)S(1)} %get-tuple-element.436, f32[64,64]{1,0:T(8,128)S(1)} %fusion.240, f32[64,64]{1,0:T(8,128)S(1)} %get-tuple-element.435, f32[64,128]{1,0:T(8,128)S(1)} %get-tuple-element.440, ...), kind=kLoop, calls=%fused_computation.55.clone.1 | loop fusion | flops 12566528 | bytes 197120 | tf_op jit(solution)/shard_map/while/body/eval_jaxpr/transpose(jvp())/reduce_sum | solution.py:36
  355.1 11.7 %fusion.241 = (f32[64,64]{1,0:T(8,128)S(1)}, f32[64,64]{1,0:T(8,128)S(1)}, f32[64,64]{1,0:T(8,128)S(1)}, f32[64,64]{1,0:T(8,128)S(1)}) fusion(f32[64,128]{1,0:T(8,128)S(1)} %get-tuple-element.436, f32[64,64]{1,0:T(8,128)S(1)} %fusion.240, f32[64,64]{1,0:T(8,128)S(1)} %get-tuple-element.435, f32[64,128]{1,0:T(8,128)S(1)} %get-tuple-element.440, ...), kind=kLoop, calls=%fused_computation.55.clone.1 | loop fusion | flops 12566528 | bytes 197120 | tf_op jit(solution)/shard_map/while/body/eval_jaxpr/transpose(jvp())/reduce_sum | solution.py:36
  370.8 11.7 %fusion.241 = (f32[64,64]{1,0:T(8,128)S(1)}, f32[64,64]{1,0:T(8,128)S(1)}, f32[64,64]{1,0:T(8,128)S(1)}, f32[64,64]{1,0:T(8,128)S(1)}) fusion(f32[64,128]{1,0:T(8,128)S(1)} %get-tuple-element.436, f32[64,64]{1,0:T(8,128)S(1)} %fusion.240, f32[64,64]{1,0:T(8,128)S(1)} %get-tuple-element.435, f32[64,128]{1,0:T(8,128)S(1)} %get-tuple-element.440, ...), kind=kLoop, calls=%fused_computation.55.clone.1 | loop fusion | flops 12566528 | bytes 197120 | tf_op jit(solution)/shard_map/while/body/eval_jaxpr/transpose(jvp())/reduce_sum | solution.py:36
  386.6 11.7 %fusion.241 = (f32[64,64]{1,0:T(8,128)S(1)}, f32[64,64]{1,0:T(8,128)S(1)}, f32[64,64]{1,0:T(8,128)S(1)}, f32[64,64]{1,0:T(8,128)S(1)}) fusion(f32[64,128]{1,0:T(8,128)S(1)} %get-tuple-element.436, f32[64,64]{1,0:T(8,128)S(1)} %fusion.240, f32[64,64]{1,0:T(8,128)S(1)} %get-tuple-element.435, f32[64,128]{1,0:T(8,128)S(1)} %get-tuple-element.440, ...), kind=kLoop, calls=%fused_computation.55.clone.1 | loop fusion | flops 12566528 | bytes 197120 | tf_op jit(solution)/shard_map/while/body/eval_jaxpr/transpose(jvp())/reduce_sum | solution.py:36
  402.3 11.7 %fusion.241 = (f32[64,64]{1,0:T(8,128)S(1)}, f32[64,64]{1,0:T(8,128)S(1)}, f32[64,64]{1,0:T(8,128)S(1)}, f32[64,64]{1,0:T(8,128)S(1)}) fusion(f32[64,128]{1,0:T(8,128)S(1)} %get-tuple-element.436, f32[64,64]{1,0:T(8,128)S(1)} %fusion.240, f32[64,64]{1,0:T(8,128)S(1)} %get-tuple-element.435, f32[64,128]{1,0:T(8,128)S(1)} %get-tuple-element.440, ...), kind=kLoop, calls=%fused_computation.55.clone.1 | loop fusion | flops 12566528 | bytes 197120 | tf_op jit(solution)/shard_map/while/body/eval_jaxpr/transpose(jvp())/reduce_sum | solution.py:36
  418.0 11.7 %fusion.241 = (f32[64,64]{1,0:T(8,128)S(1)}, f32[64,64]{1,0:T(8,128)S(1)}, f32[64,64]{1,0:T(8,128)S(1)}, f32[64,64]{1,0:T(8,128)S(1)}) fusion(f32[64,128]{1,0:T(8,128)S(1)} %get-tuple-element.436, f32[64,64]{1,0:T(8,128)S(1)} %fusion.240, f32[64,64]{1,0:T(8,128)S(1)} %get-tuple-element.435, f32[64,128]{1,0:T(8,128)S(1)} %get-tuple-element.440, ...), kind=kLoop, calls=%fused_computation.55.clone.1 | loop fusion | flops 12566528 | bytes 197120 | tf_op jit(solution)/shard_map/while/body/eval_jaxpr/transpose(jvp())/reduce_sum | solution.py:36
  435.6 81.9 %all-reduce = (f32[512]{0:T(512)}, f32[512]{0:T(512)}) all-reduce(f32[512]{0:T(512)S(1)} %reshape.694, f32[512]{0:T(512)S(1)} %get-tuple-element.272), channel_id=1, replica_groups=mesh['dp'=4,'ctx'=64] {'dp','ctx'}, use_global_device_ids=true, to_apply=%region_11.12 | all-reduce | flops 1024 | bytes 8192 | tf_op jit(solution)/shard_map/psum | solution.py:193
  517.5 173.0 %all-reduce.4.cloned.1.call-done = (f32[512,64]{0,1:T(8,128)}, f32[512,64]{0,1:T(8,128)}, f32[512,64]{0,1:T(8,128)}, f32[512,64]{0,1:T(8,128)}) async-done(((f32[512,64]{0,1:T(8,128)}, f32[512,64]{0,1:T(8,128)}, f32[512,64]{0,1:T(8,128)}, f32[512,64]{0,1:T(8,128)}), (f32[512,64]{0,1:T(8,128)}, f32[512,64]{0,1:T(8,128)}, f32[512,64]{0,1:T(8,128)}, f32[512,64]{0,1:T(8,128)})) %all-reduce.4.cloned.1.call-update) | async-done | bytes 524304 | tf_op jit(solution)/shard_map/psum | solution.py:193
  690.6 1.6 copy.251
  (224 shorter events, 73.9 us)
Async XLA Ops:
  7.2 4.2 copy-start.10
  11.4 90.0 %copy-start.6 = (bf16[1,128,512]{2,1,0:T(8,128)(2,1)S(1)}, bf16[1,128,512]{2,1,0:T(8,128)(2,1)}, u32[]{:S(2)}) copy-start(bf16[1,128,512]{2,1,0:T(8,128)(2,1)} %param.12) | copy-start | bytes 393220
  85.0 20.3 %copy-start = (f32[8,64,64]{2,1,0:T(8,128)}, f32[8,64,64]{2,1,0:T(8,128)S(1)}, u32[]{:S(2)}) copy-start(f32[8,64,64]{2,1,0:T(8,128)S(1)} %get-tuple-element.545) | copy-start | bytes 393220
  85.0 20.3 %copy-start.3 = (f32[8,64,64]{2,1,0:T(8,128)}, f32[8,64,64]{2,1,0:T(8,128)S(1)}, u32[]{:S(2)}) copy-start(f32[8,64,64]{2,1,0:T(8,128)S(1)} %get-tuple-element.548) | copy-start | bytes 393220
  85.0 20.3 %copy-start.4 = (f32[8,64,64]{2,1,0:T(8,128)}, f32[8,64,64]{2,1,0:T(8,128)S(1)}, u32[]{:S(2)}) copy-start(f32[8,64,64]{2,1,0:T(8,128)S(1)} %get-tuple-element.549) | copy-start | bytes 393220
  85.0 18.7 %copy-start.7 = (bf16[1,128,512]{2,1,0:T(8,128)(2,1)S(1)}, bf16[1,128,512]{2,1,0:T(8,128)(2,1)}, u32[]{:S(2)}) copy-start(bf16[1,128,512]{2,1,0:T(8,128)(2,1)} %param.13) | copy-start | bytes 393220
  87.9 23.5 %all-to-all-start.2 = ((bf16[64,2,512]{2,1,0:T(2,128)(2,1)}), bf16[64,2,512]{2,1,0:T(2,128)(2,1)S(1)}, u32[]{:S(2)}, u32[]{:S(2)}) async-start(bf16[64,2,512]{2,1,0:T(2,128)(2,1)} %reshape.721), calls=%async_computation.2 | async-start | bytes 262144 | tf_op jit(solution)/shard_map/all_to_all | solution.py:171
  111.4 15.5 %all-to-all-start = ((bf16[64,2,512]{2,1,0:T(2,128)(2,1)}), bf16[64,2,512]{2,1,0:T(2,128)(2,1)S(1)}, u32[]{:S(2)}, u32[]{:S(2)}) async-start(bf16[64,2,512]{2,1,0:T(2,128)(2,1)} %reshape.717), calls=%async_computation | async-start | bytes 262144 | tf_op jit(solution)/shard_map/all_to_all | solution.py:167
  126.8 15.1 %all-to-all-start.1 = ((bf16[64,2,512]{2,1,0:T(2,128)(2,1)}), bf16[64,2,512]{2,1,0:T(2,128)(2,1)S(1)}, u32[]{:S(2)}, u32[]{:S(2)}) async-start(bf16[64,2,512]{2,1,0:T(2,128)(2,1)} %reshape.719), calls=%async_computation.1 | async-start | bytes 262144 | tf_op jit(solution)/shard_map/all_to_all | solution.py:168
  142.9 1.0 copy-start.5
  148.4 39.5 %all-to-all-start.3 = ((f32[3,128,2,512]{3,2,0,1:T(2,128)}), f32[3,128,2,512]{3,2,0,1:T(2,128)S(1)}, u32[]{:S(2)}, u32[]{:S(2)}) async-start(f32[3,128,2,512]{3,2,0,1:T(2,128)} %copy.162), calls=%async_computation.3 | async-start | bytes 3145728 | tf_op jit(solution)/shard_map/all_to_all | solution.py:105
  187.9 42.5 %all-to-all-start.4 = ((f32[3,128,2,512]{3,2,0,1:T(2,128)}), f32[3,128,2,512]{3,2,0,1:T(2,128)S(1)}, u32[]{:S(2)}, u32[]{:S(2)}) async-start(f32[3,128,2,512]{3,2,0,1:T(2,128)} %copy.166), calls=%async_computation.4 | async-start | bytes 3145728 | tf_op jit(solution)/shard_map/all_to_all | solution.py:106
  234.9 1.7 copy-start.2
  243.9 21.5 %all-to-all-start.5 = ((bf16[1,2,128,1024]{3,1,0,2:T(2,128)(2,1)}), bf16[1,2,128,1024]{3,1,0,2:T(2,128)(2,1)S(1)}, u32[]{:S(2)}, u32[]{:S(2)}) async-start(bf16[1,2,128,1024]{3,1,0,2:T(2,128)(2,1)} %copy.172), calls=%async_computation.5 | async-start | bytes 1048576 | tf_op jit(solution)/shard_map/all_to_all | solution.py:133
  265.4 18.6 %all-to-all-start.6 = ((bf16[1,2,128,1024]{3,1,0,2:T(2,128)(2,1)}), bf16[1,2,128,1024]{3,1,0,2:T(2,128)(2,1)S(1)}, u32[]{:S(2)}, u32[]{:S(2)}) async-start(bf16[1,2,128,1024]{3,1,0,2:T(2,128)(2,1)} %copy.175), calls=%async_computation.6 | async-start | bytes 1048576 | tf_op jit(solution)/shard_map/all_to_all | solution.py:136
  287.4 18.2 %copy-start.8 = (bf16[1,128,512]{2,1,0:T(8,128)(2,1)S(1)}, bf16[1,128,512]{2,1,0:T(8,128)(2,1)}, u32[]{:S(2)}) copy-start(bf16[1,128,512]{2,1,0:T(8,128)(2,1)} %param.13) | copy-start | bytes 393220
  287.4 18.2 %copy-start.9 = (f32[512]{0:T(512)S(1)}, f32[512]{0:T(512)}, u32[]{:S(2)}) copy-start(f32[512]{0:T(512)} %param.19) | copy-start | bytes 6148
  289.4 17.1 %copy-start.1 = (f32[8,64,64]{2,1,0:T(8,128)S(1)}, f32[8,64,64]{2,1,0:T(8,128)}, u32[]{:S(2)}) copy-start(f32[8,64,64]{2,1,0:T(8,128)} %copy-done) | copy-start | bytes 393220
  289.4 16.1 %all-to-all-start.7 = ((bf16[1,64,2,1024]{3,2,0,1:T(2,128)(2,1)}), bf16[1,64,2,1024]{3,2,0,1:T(2,128)(2,1)S(1)}, u32[]{:S(2)}, u32[]{:S(2)}) async-start(bf16[1,64,2,1024]{3,2,0,1:T(2,128)(2,1)} %copy.180), calls=%async_computation.7 | async-start | bytes 524288 | tf_op jit(solution)/shard_map/all_to_all | solution.py:153
  294.6 396.0 %all-reduce.4.cloned.1.call-start = ((), (), s32[]{:S(2)}) async-start(), calls=%async_computation.8 | async-start | bytes 1048576 | tf_op jit(solution)/shard_map/psum | solution.py:193
Sparse Core Ops, SparseCore 0:
  435.6 254.8 all-reduce.3
where the time goes:
time: 714 us; the launch traced here: 704 us
  waiting for transfers between devices  289 us (40%)
  other arithmetic  205 us (29%)
  blocking collectives  81.9 us (11%)
  starting transfers between devices  55.6 us (8%)
  local copies, waits for them, and re-layouts  39.1 us (5%)
  matrix products  18.1 us (3%)
  between operations  15.1 us (2%)
    psum x1, waiting for transfers between devices, body(): lax.psum((pulled[0], pulled[1], pulled[2], pulled[3], pulled[4], skip_par...  173 us
    reduce_sum x8, other arithmetic, kernel_block(): decays = jnp.exp(w_re[:, :, None] * positions)  93.4 us
    psum x1, blocking collectives, body(): lax.psum((pulled[0], pulled[1], pulled[2], pulled[3], pulled[4], skip_par...  81.9 us
    reduce_sum x8, other arithmetic, kernel_block(): jnp.sum(ct_re[:, :, None] * wave_re - ct_im[:, :, None] * wave_im, axis=1)  70 us
    all_to_all x1, waiting for transfers between devices, spectrum(): lax.all_to_all(twisted_re, 'ctx', split_axis=1, concat_axis=2, tiled=True)  32.6 us
    all_to_all x1, waiting for transfers between devices, spectrum(): lax.all_to_all(twisted_im, 'ctx', split_axis=1, concat_axis=2, tiled=True)  27.1 us
  transfers between devices with their start and end apart: 9, of which 9 were waited for; matrix products, arithmetic and copies ran while one was open for 3% of the time, Pallas kernels for 0%

commit v1 on v0

v1 whole, which is shorter than its diff:
```python
import functools

import jax
import jax.numpy as jnp
from jax import lax
from jax.experimental import pallas as pl
from jax.experimental.pallas import tpu as pltpu
from jax.sharding import PartitionSpec as P

AXES = ("dp", "ctx")
F32 = jnp.float32
BF16 = jnp.bfloat16
ROWS_IN = 4
ROWS_OUT = 8
FLIP = (((1,), (1,)), ((), ()))
PLAIN = (((1,), (0,)), ((), ()))
OUTER = (((0,), (0,)), ((), ()))


def halves(value):
    high = value.astype(BF16)
    low = (value - high.astype(F32)).astype(BF16)
    return (high, low)


def dot(a, b, dims):
    return lax.dot_general(a, b, dims, preferred_element_type=F32)


def send_kernel(inputs_ref, grad_ref, out_ref, rows):
    owners = rows.shape[0] // ROWS_IN
    for part, ref in enumerate((inputs_ref, grad_ref)):
        block = ref[...].astype(F32)
        for half in range(2):
            piece = block[:, half * owners : (half + 1) * owners].T
            rows[pl.ds(2 * part + half, owners, stride=ROWS_IN), :] = piece
    out_ref[...] = rows[...].astype(BF16)


def table_kernel(cols_ref, fwd_hi, fwd_lo, rev_hi, rev_lo, mix_hi, mix_lo, band_hi, band_lo):
    poles = cols_ref.shape[0]
    half = poles // 2
    span = poles
    w_re, w_im = cols_ref[:, 0:1], cols_ref[:, 1:2]
    ct_re, ct_im = cols_ref[:, 2:3], cols_ref[:, 3:4]
    lane = lax.broadcasted_iota(jnp.int32, (poles, span), 1)
    sub = lax.broadcasted_iota(jnp.int32, (poles, span), 0)
    first = sub < half

    def spread(value):
        return jnp.concatenate([jnp.where(first, value, 0.0), jnp.where(first, 0.0, value)], axis=1)

    def put(hi_ref, lo_ref, part, value):
        hi, lo = halves(spread(value))
        hi_ref[part * poles : (part + 1) * poles, :] = hi
        lo_ref[part * poles : (part + 1) * poles, :] = lo

    step = lane.astype(F32)
    grow = jnp.exp(w_re * step)
    turn = w_im * step
    f_re, f_im = grow * jnp.cos(turn), grow * jnp.sin(turn)
    put(fwd_hi, fwd_lo, 0, f_re)
    put(fwd_hi, fwd_lo, 1, f_im)
    put(fwd_hi, fwd_lo, 2, f_re * step)
    put(fwd_hi, fwd_lo, 3, f_im * step)
    back = (span - lane).astype(F32)
    shrink = jnp.exp(w_re * back)
    twist = w_im * back
    h_re, h_im = shrink * jnp.cos(twist), shrink * jnp.sin(twist)
    put(rev_hi, rev_lo, 0, h_re)
    put(rev_hi, rev_lo, 1, h_im)
    put(rev_hi, rev_lo, 2, h_re * back)
    put(rev_hi, rev_lo, 3, h_im * back)
    put(mix_hi, mix_lo, 0, 2.0 * (ct_re * h_re - ct_im * h_im))
    put(mix_hi, mix_lo, 1, -2.0 * (ct_re * h_im + ct_im * h_re))
    taps = 2.0 * (ct_re * f_re - ct_im * f_im)
    upper = lane >= sub
    zero = jnp.zeros((span, span), F32)
    for chan in range(2):
        line = jnp.sum(taps[chan * half : (chan + 1) * half, :], axis=0, keepdims=True)
        band = pltpu.roll(jnp.broadcast_to(line, (span, span)), 0, 1, stride=1, stride_axis=0)
        band = jnp.where(upper, band, 0.0)
        wide = jnp.concatenate([band, zero] if chan == 0 else [zero, band], axis=1)
        hi, lo = halves(wide)
        band_hi[chan * span : (chan + 1) * span, :] = hi
        band_lo[chan * span : (chan + 1) * span, :] = lo


def skew(value):
    size = value.shape[0]
    sub = lax.broadcasted_iota(jnp.int32, value.shape, 0)
    lane = lax.broadcasted_iota(jnp.int32, value.shape, 1)
    value = jnp.where(lane >= sub, value, 0.0)
    bit = 1
    while bit < size:
        value = jnp.where((sub & bit) != 0, pltpu.roll(value, size - bit, 1), value)
        bit *= 2
    return value


def core_kernel(
    batch,
    recv_ref,
    fwd_hi,
    fwd_lo,
    rev_hi,
    rev_lo,
    mix_hi,
    mix_lo,
    band_hi,
    band_lo,
    prm_ref,
    out_ref,
    rows,
    g_re,
    g_im,
    d_re,
    d_im,
    z_re,
    z_im,
    y_re,
    y_im,
    outs,
):
    sources = rows.shape[0] // ROWS_IN
    chunks = sources // batch
    poles = prm_ref.shape[1]
    span = poles
    half = poles // 2
    rows[...] = recv_ref[...].astype(F32)

    def part(index):
        return rows[pl.ds(index, sources, stride=ROWS_IN), :]

    u_f = jnp.concatenate([part(0), part(1)], axis=1)
    g_f = jnp.concatenate([part(2), part(3)], axis=1)
    u_b, g_b = u_f.astype(BF16), g_f.astype(BF16)
    moments = dot(g_b, fwd_hi[...], FLIP) + dot(g_b, fwd_lo[...], FLIP)
    for index, ref in enumerate((g_re, g_im, d_re, d_im)):
        ref[...] = moments[:, index * poles : (index + 1) * poles]
    prm = prm_ref[...]

    def line(index):
        return prm[index : index + 1, :]

    e_re, e_im = line(0), line(1)
    a, b, c, d = (jnp.zeros((batch, poles), F32) for _ in range(4))
    for chunk in reversed(range(chunks)):
        at = pl.ds(chunk, batch, stride=chunks)
        z_re[at, :] = a
        z_im[at, :] = b
        y_re[at, :] = c
        y_im[at, :] = d
        if chunk > 0:
            m = c + span * a
            n = d + span * b
            a, b = (e_re * a - e_im * b) + g_re[at, :], (e_re * b + e_im * a) + g_im[at, :]
            c, d = (e_re * m - e_im * n) + d_re[at, :], (e_re * n + e_im * m) + d_im[at, :]
    lead = dot(u_b, rev_hi[...], FLIP) + dot(u_b, rev_lo[...], FLIP)
    v_re, v_im = lead[:, :poles], lead[:, poles : 2 * poles]
    x_re, x_im = lead[:, 2 * poles : 3 * poles], lead[:, 3 * poles :]
    a, b, c, d = z_re[...], z_im[...], y_re[...], y_im[...]

    def total(value):
        return jnp.sum(value, axis=0, keepdims=True)

    s_re = total(v_re * a - v_im * b)
    s_im = total(v_re * b + v_im * a)
    t_re = total(x_re * a - x_im * b + v_re * c - v_im * d)
    t_im = total(x_re * b + x_im * a + v_re * d + v_im * c)

    state = jnp.concatenate([a, b], axis=1)
    state_hi, state_lo = halves(state)
    back = dot(state_hi, mix_hi[...], PLAIN) + dot(state_lo, mix_hi[...], PLAIN)
    back = back + dot(state_hi, mix_lo[...], PLAIN)
    back = back + dot(g_b, band_hi[...], FLIP) + dot(g_b, band_lo[...], FLIP)
    gain = jnp.concatenate([line(14), line(15)], axis=1)
    back = back + gain * g_f

    cross = dot(u_b, g_b, OUTER)
    lags = [
        total(skew(cross[k * span : (k + 1) * span, k * span : (k + 1) * span])) for k in range(2)
    ]
    lag = jnp.broadcast_to(jnp.concatenate(lags, axis=1), (8, 2 * span))
    lag_hi, lag_lo = halves(lag)
    near = dot(lag_hi, fwd_hi[...], FLIP) + dot(lag_lo, fwd_hi[...], FLIP)
    near = (near + dot(lag_hi, fwd_lo[...], FLIP))[0:1]
    s_re = s_re + near[:, :poles]
    s_im = s_im + near[:, poles : 2 * poles]
    t_re = t_re + near[:, 2 * poles : 3 * poles]
    t_im = t_im + near[:, 3 * poles :]

    def times(p, q):
        return (p[0] * q[0] - p[1] * q[1], p[0] * q[1] + p[1] * q[0])

    s, t = (s_re, s_im), (t_re, t_im)
    ct, lift = (line(2), line(3)), (line(4), line(5))
    slope, ratio = (line(6), line(7)), (line(8), line(9))
    size, pole_re, w = line(10), line(11), (line(12), line(13))
    by_c = times(s, lift)
    first, second = times(s, slope), times(t, ct)
    by_w = (first[0] + second[0], first[1] + second[1])
    third = times(s, ratio)
    by_a = (size * by_w[0] - third[0], size * by_w[1] - third[1])
    by_dt = 2.0 * (by_w[0] * w[0] - by_w[1] * w[1])
    lane = lax.broadcasted_iota(jnp.int32, (1, poles), 1)
    by_skip = total(u_f * g_f)
    loose = [
        jnp.sum(jnp.where(lane < half, by_dt, 0.0), axis=1, keepdims=True),
        jnp.sum(jnp.where(lane < half, 0.0, by_dt), axis=1, keepdims=True),
        jnp.sum(by_skip[:, :span], axis=1, keepdims=True),
        jnp.sum(by_skip[:, span:], axis=1, keepdims=True),
    ]
    misc = jnp.zeros((1, poles), F32)
    for index, value in enumerate(loose):
        misc = jnp.where(lane == index, value, misc)
    lines = [
        2.0 * by_a[0] * pole_re,
        -2.0 * by_a[1],
        2.0 * by_c[0],
        -2.0 * by_c[1],
        misc,
        jnp.zeros((1, poles), F32),
    ]
    outs[pl.ds(0, sources, stride=ROWS_OUT), :] = back[:, :span]
    outs[pl.ds(1, sources, stride=ROWS_OUT), :] = back[:, span:]
    for index, value in enumerate(lines):
        outs[pl.ds(2 + index, sources, stride=ROWS_OUT), :] = jnp.broadcast_to(
            value, (sources, poles)
        )
    out_ref[...] = outs[...].astype(BF16)


def finish_kernel(recv_ref, grad_ref, a_ref, b_ref, c_ref, d_ref, misc_ref, rows):
    owners = rows.shape[0] // ROWS_OUT
    half = a_ref.shape[0]
    rows[...] = recv_ref[...].astype(F32)

    def turned(index):
        return rows[pl.ds(index, owners, stride=ROWS_OUT), :].T

    for part in range(2):
        grad_ref[:, part * owners : (part + 1) * owners] = turned(part).astype(BF16)
    for index, ref in enumerate((a_ref, b_ref, c_ref, d_ref)):
        block = turned(2 + index)
        ref[:, :owners] = block[:half]
        ref[:, owners:] = block[half:]
    misc_ref[...] = turned(6)[0:8]


def pole_lines(step_size, pole_re, a_im, c_re, c_im):
    w_re = step_size * pole_re
    w_im = step_size * a_im
    growth = jnp.exp(w_re)
    cosine, sine = jnp.cos(w_im), jnp.sin(w_im)
    half_sin = jnp.sin(0.5 * w_im)
    e_re = jnp.expm1(w_re) * cosine - 2.0 * half_sin * half_sin
    e_im = growth * sine
    modulus = pole_re * pole_re + a_im * a_im

    def over_pole(re, im):
        return ((re * pole_re + im * a_im) / modulus, (im * pole_re - re * a_im) / modulus)

    ct_re, ct_im = over_pole(e_re * c_re - e_im * c_im, e_re * c_im + e_im * c_re)
    lift = over_pole(e_re, e_im)
    g_re, g_im = growth * cosine, growth * sine
    slope = over_pole(g_re * c_re - g_im * c_im, g_re * c_im + g_im * c_re)
    ratio = over_pole(ct_re, ct_im)
    return (w_re, w_im, ct_re, ct_im) + lift + slope + ratio


def vmem(count):
    return [pl.BlockSpec(memory_space=pltpu.VMEM)] * count


def body(inputs, grad_out, log_dt, log_a_re, a_im, c_re, c_im, skip_gain):
    batch = lax.axis_size("dp")
    devices = batch * lax.axis_size("ctx")
    span, channels = inputs.shape[1:]
    poles = a_im.shape[1]
    assert channels == 2 * devices and span == 2 * poles
    place = lax.axis_index(AXES)

    sent = pl.pallas_call(
        send_kernel,
        out_shape=jax.ShapeDtypeStruct((devices * ROWS_IN, span), BF16),
        in_specs=vmem(2),
        out_specs=vmem(1)[0],
        scratch_shapes=[pltpu.VMEM((devices * ROWS_IN, span), F32)],
    )(inputs[0], grad_out[0])
    recv = lax.all_to_all(
        sent.reshape(devices, ROWS_IN, span), AXES, split_axis=0, concat_axis=0, tiled=True
    ).reshape(devices * ROWS_IN, span)

    def own(value):
        turned = value.T
        pair = [
            lax.dynamic_slice_in_dim(turned, place + k * devices, 1, axis=1) for k in range(2)
        ]
        return jnp.concatenate(pair, axis=0)[:, 0]

    def own_flat(value):
        pair = [lax.dynamic_slice_in_dim(value, place + k * devices, 1) for k in range(2)]
        return jnp.repeat(jnp.concatenate(pair), poles)

    step_size = jnp.exp(own_flat(log_dt))
    pole_re = -jnp.exp(own(log_a_re))
    im = own(a_im)
    terms = pole_lines(step_size, pole_re, im, own(c_re), own(c_im))
    w_re, w_im, ct_re, ct_im = terms[:4]
    far = jnp.exp(w_re * span)
    gains = [
        jnp.broadcast_to(lax.dynamic_slice_in_dim(skip_gain, place + k * devices, 1), (span,))
        for k in range(2)
    ]
    prm = jnp.stack(
        [far * jnp.cos(w_im * span), far * jnp.sin(w_im * span)]
        + list(terms[2:])
        + [step_size, pole_re, w_re, w_im]
        + gains
    )
    cols = jnp.stack([w_re, w_im, ct_re, ct_im], axis=1)
    wide = 2 * span
    tall = jax.ShapeDtypeStruct((4 * 2 * poles, wide), BF16)
    square = jax.ShapeDtypeStruct((wide, wide), BF16)
    tables = pl.pallas_call(
        table_kernel,
        out_shape=[tall] * 4 + [square] * 4,
        in_specs=vmem(1),
        out_specs=vmem(8),
    )(cols)
    grid = pltpu.VMEM((devices, span), F32)
    answer = pl.pallas_call(
        functools.partial(core_kernel, batch),
        out_shape=jax.ShapeDtypeStruct((devices * ROWS_OUT, span), BF16),
        in_specs=vmem(10),
        out_specs=vmem(1)[0],
        scratch_shapes=[pltpu.VMEM((devices * ROWS_IN, span), F32)]
        + [grid] * 8
        + [pltpu.VMEM((devices * ROWS_OUT, span), F32)],
    )(recv, *tables, prm)
    back = lax.all_to_all(
        answer.reshape(devices, ROWS_OUT, span), AXES, split_axis=0, concat_axis=0, tiled=True
    ).reshape(devices * ROWS_OUT, span)
    line = jax.ShapeDtypeStruct((poles, channels), F32)
    results = pl.pallas_call(
        finish_kernel,
        out_shape=[jax.ShapeDtypeStruct((span, channels), BF16)]
        + [line] * 4
        + [jax.ShapeDtypeStruct((8, devices), F32)],
        in_specs=vmem(1),
        out_specs=vmem(6),
        scratch_shapes=[pltpu.VMEM((devices * ROWS_OUT, span), F32)],
    )(back)
    misc = results[5]
    return (
        results[0][None],
        misc[0:2].reshape(channels),
        results[1].T,
        results[2].T,
        results[3].T,
        results[4].T,
        misc[2:4].reshape(channels),
    )


def solution(mesh):
    placed = (P("dp", "ctx", None), P("dp", "ctx", None), P(), P(), P(), P(), P(), P())
    return jax.shard_map(
        body,
        mesh=mesh,
        in_specs=placed,
        out_specs=(P("dp", "ctx", None), P(), P(), P(), P(), P(), P()),
        check_vma=False,
    )
```

time: 714 us -> 71.7 us (0.10); the launches traced: 704 us -> 71.3 us
  waiting for transfers between devices: 289 us -> 6.38 us
  other arithmetic: 205 us -> 1.81 us
  blocking collectives: 81.9 us -> 28.3 us
  starting transfers between devices: 55.6 us -> 15.7 us
  local copies, waits for them, and re-layouts: 39.1 us -> 7.26 us
  matrix products: 18.1 us -> 0 us
  between operations: 15.1 us -> 0.78 us
  Pallas kernels: 0 us -> 11.1 us
    psum x1 -> x0, waiting for transfers between devices: 173 us -> none  [body(): lax.psum((pulled[0], pulled[1], pulled[2], pulled[3], pulled[4], skip_par...]
    reduce_sum x24 -> x0, other arithmetic: 172 us -> none  [the longest x8 93.4 us: kernel_block(): decays = jnp.exp(w_re[:, :, None] * positions)]
    all_to_all x8 -> x1, waiting for transfers between devices: 115 us -> 6.38 us  [body(): lax.all_to_all(sent.reshape(devices, ROWS_IN, span), AXES, split_axis=0,...]
    psum x1 -> x0, blocking collectives: 81.9 us -> none  [body(): lax.psum((pulled[0], pulled[1], pulled[2], pulled[3], pulled[4], skip_par...]
    all_to_all x8 -> x1, starting transfers between devices: 55.3 us -> 15.7 us  [body(): lax.all_to_all(sent.reshape(devices, ROWS_IN, span), AXES, split_axis=0,...]
    all_to_all x0 -> x1, blocking collectives: none -> 28.3 us  [body(): lax.all_to_all(answer.reshape(devices, ROWS_OUT, span), AXES, split_axis=...]
    dot_general x12 -> x0, matrix products: 18.1 us -> none  [the longest x1 2.78 us: spectrum(): jnp.einsum('kn,sanh->sakh', cos_two, rows_re, precision=HIGHEST)]
    dynamic_update_slice x24 -> x0, other arithmetic: 12.4 us -> none  [the longest x16 12.2 us: kernel_pullback(): pulled = lax.map(one_block, grouped + (cot_blocks,))]
  transfers between devices with their start and end apart: 9 -> 1, of which waited for: 9 -> 1; matrix products, arithmetic and copies ran while one was open for 3% -> 9% of each run, Pallas kernels for 0% -> 4%
where the time goes in v1:
time: 71.7 us; the launch traced here: 71.3 us
  blocking collectives  28.3 us (39%)
  starting transfers between devices  15.7 us (22%)
  Pallas kernels  11.1 us (15%)
  local copies, waits for them, and re-layouts  7.26 us (10%)
  waiting for transfers between devices  6.38 us (9%)
  other arithmetic  1.81 us (3%)
  between operations  0.78 us (1%)
    all_to_all x1, blocking collectives, body(): lax.all_to_all(answer.reshape(devices, ROWS_OUT, span), AXES, split_axis=...  28.3 us
    all_to_all x1, starting transfers between devices, body(): lax.all_to_all(sent.reshape(devices, ROWS_IN, span), AXES, split_axis=0,...  15.7 us
    all_to_all x1, waiting for transfers between devices, body(): lax.all_to_all(sent.reshape(devices, ROWS_IN, span), AXES, split_axis=0,...  6.38 us
    pallas_call x1, Pallas kernels, body(): pl.pallas_call(functools.partial(core_kernel, batch), out_shape=jax.Shape...  4.56 us
    unnamed x17, local copies, waits for them, and re-layouts  2.66 us
    pallas_call x1, Pallas kernels, body(): pl.pallas_call(table_kernel, out_shape=[tall] * 4 + [square] * 4, in_spec...  2.66 us
    another operation x3, local copies, waits for them, and re-layouts, body(): jnp.stack([far * jnp.cos(w_im * span), far * jnp.sin(w_im * span)] + list...  2.52 us
    pallas_call x1, Pallas kernels, body(): pl.pallas_call(finish_kernel, out_shape=[jax.ShapeDtypeStruct((span, chan...  2.04 us
  transfers between devices with their start and end apart: 1, of which 1 were waited for; matrix products, arithmetic and copies ran while one was open for 9% of the time, Pallas kernels for 4%

profile of v1, /device:TPU:1, one launch (start us, length us, event | category | flops | bytes accessed | tf_op | source)
XLA Modules:
  0.0 71.3 jit_solution(9249447790390135347)
XLA Ops:
  0.6 1.8 %shard_map.135 = bf16[1024,128]{1,0:T(8,128)(2,1)} custom-call(bf16[128,512]{1,0:T(8,128)(2,1)} %bitcast.157, bf16[128,512]{1,0:T(8,128)(2,1)} %bitcast.158), custom_call_target="tpu_custom_call" | custom-call | tf_op jit(solution)/shard_map/pallas_call | solution.py:284
  2.5 0.0 copy-start.5
  2.5 0.0 copy-start.6
  2.5 0.0 copy-start.1
  2.5 0.0 copy-start.2
  2.5 0.0 copy-start.4
  2.5 15.7 %all-to-all-start = ((bf16[256,4,128]{2,1,0:T(4,128)(2,1)}), bf16[256,4,128]{2,1,0:T(4,128)(2,1)S(1)}, u32[]{:S(2)}, u32[]{:S(2)}) async-start(bf16[256,4,128]{2,1,0:T(4,128)(2,1)} %bitcast.156), calls=%async_computation | async-start | bytes 524288 | tf_op jit(solution)/shard_map/all_to_all | solution.py:291
  18.2 0.0 copy-start.3
  18.2 0.0 copy-done.5
  18.2 0.0 copy-done.6
  18.2 0.6 fusion.28
  18.8 1.4 %maximum_exponential_fusion = f32[2]{0:T(128)S(1)} fusion(f32[1]{0:T(128)} %get-tuple-element.82, f32[1]{0:T(128)} %get-tuple-element.83), kind=kLoop, calls=%fused_computation.15 | loop fusion | flops 2 | bytes 16 | tf_op jit(solution)/shard_map/exp | solution.py:306
  20.2 0.1 broadcast_in_dim.6
  20.2 0.1 exp.224
  20.3 0.1 exp.221
  20.4 0.0 copy-done.1
  20.4 0.0 copy-done.2
  20.4 0.2 dynamic-slice_reduce_fusion.5
  20.7 0.0 copy-done.4
  20.7 0.0 copy-done.3
  20.7 0.2 dynamic-slice_reduce_fusion.1
  20.9 0.1 negate_bitcast_fusion
  21.0 0.1 fusion.27
  21.1 0.1 fusion.17
  21.2 0.1 fusion.13
  21.3 0.1 add_divide_fusion
  21.4 0.7 %copy.35.cols_ref = f32[128,4]{1,0:T(8,128)} copy(f32[128,4]{0,1:T(4,128)S(1)} %pad_maximum_fusion) | data formatting | bytes 4096 | tf_op jit(solution)/shard_map/stack | solution.py:322
  22.1 2.7 %shard_map.136 = (bf16[512,256]{1,0:T(8,128)(2,1)}, bf16[512,256]{1,0:T(8,128)(2,1)}, bf16[512,256]{1,0:T(8,128)(2,1)}, bf16[512,256]{1,0:T(8,128)(2,1)}, bf16[2...) custom-call(f32[128,4]{1,0:T(8,128)} %copy.35.cols_ref), custom_call_target="tpu_custom_call" | custom-call | tf_op jit(solution)/shard_map/pallas_call | solution.py:326
  24.8 0.6 stack_broadcast_in_dim.5
  25.5 0.6 stack_broadcast_in_dim.4
  26.1 1.2 %stack.5.prm_ref = f32[16,128]{1,0:T(8,128)} concatenate(f32[1,128]{1,0:T(1,128)S(1)} %get-tuple-element.77, f32[1,128]{1,0:T(1,128)S(1)} %get-tuple-element.76, f32[1,128]{1,0:T(1,128)S(1)} %get-tuple-element.47, f32[1,128]{1,0:T(1,128)S(1)} %get-tuple-element.46, f32[1,128]{1,0:T(1,128)S(1)} %get-tuple-element.74, f32[1,128]{1,0:T(1,128)S(1)} %get-tuple-element.55, ...), dimensions={0} | concatenate | bytes 16384 | tf_op jit(solution)/shard_map/stack | solution.py:316
  27.4 6.4 %all-to-all-done = bf16[256,4,128]{2,1,0:T(4,128)(2,1)S(1)} async-done(((bf16[256,4,128]{2,1,0:T(4,128)(2,1)}), bf16[256,4,128]{2,1,0:T(4,128)(2,1)S(1)}, u32[]{:S(2)}, u32[]{:S(2)}) %all-to-all-start) | async-done | bytes 262176 | tf_op jit(solution)/shard_map/all_to_all | solution.py:291
  33.7 0.0 copy-start
  33.7 0.7 copy-done
  34.4 4.6 %shard_map.137 = bf16[2048,128]{1,0:T(8,128)(2,1)} custom-call(bf16[1024,128]{1,0:T(8,128)(2,1)} %bitcast.155, bf16[512,256]{1,0:T(8,128)(2,1)} %get-tuple-element.21.fwd_hi, bf16[512,256]{1,0:T(8,128)(2,1)} %get-tuple-element.22.fwd_lo, bf16[512,256]{1,0:T(8,128)(2,1)} %get-tuple-element.23.rev_hi, bf16[512,256]{1,0:T(8,128)(2,1)} %get-tuple-element.24.rev_lo, ...), custom_call_target="tpu_custom_call" | custom-call | tf_op jit(solution)/shard_map/pallas_call | solution.py:333
  39.0 28.3 %all_to_all.10 = bf16[256,8,128]{2,1,0:T(8,128)(2,1)} all-to-all(bf16[256,8,128]{2,1,0:T(8,128)(2,1)} %bitcast.154), channel_id=1, replica_groups=mesh['dp'=4,'ctx'=64] {'dp','ctx'}, dimensions={0} | all-to-all | bytes 1048576 | tf_op jit(solution)/shard_map/all_to_all | solution.py:342
  67.3 2.0 %shard_map.138 = (bf16[128,512]{1,0:T(8,128)(2,1)}, f32[64,512]{1,0:T(8,128)}, f32[64,512]{1,0:T(8,128)}, f32[64,512]{1,0:T(8,128)}, f32[64,512]{1,0:T(8,128)}, /*index=5*/f32[8,256]{1,0:T(8,128)}) custom-call(bf16[2048,128]{1,0:T(8,128)(2,1)} %bitcast.153), custom_call_target="tpu_custom_call" | custom-call | tf_op jit(solution)/shard_map/pallas_call | solution.py:346
  69.3 0.8 %slice_bitcast_fusion = (f32[1,2,2,128]{3,2,1,0:T(2,128)S(1)}, f32[1,2,2,128]{3,2,1,0:T(2,128)S(1)}) fusion(f32[8,256]{1,0:T(8,128)} %get-tuple-element.30), kind=kLoop, calls=%fused_computation.9 | loop fusion | bytes 8192
  70.1 0.6 copy.37
  70.7 0.6 copy.36
  (5 shorter events, 0.1 us)
Async XLA Ops:
  2.5 15.7 %copy-start.5 = (f32[512]{0:T(512)S(1)}, f32[512]{0:T(512)}, u32[]{:S(2)}) copy-start(f32[512]{0:T(512)} %param.15) | copy-start | bytes 6148
  2.5 15.7 %copy-start.6 = (f32[512]{0:T(512)S(1)}, f32[512]{0:T(512)}, u32[]{:S(2)}) copy-start(f32[512]{0:T(512)} %param.10) | copy-start | bytes 6148
  2.5 17.9 %copy-start.1 = (f32[512,64]{0,1:T(8,128)S(1)}, f32[512,64]{0,1:T(8,128)}, u32[]{:S(2)}) copy-start(f32[512,64]{0,1:T(8,128)} %param.12) | copy-start | bytes 393220
  2.5 17.9 %copy-start.2 = (f32[512,64]{0,1:T(8,128)S(1)}, f32[512,64]{0,1:T(8,128)}, u32[]{:S(2)}) copy-start(f32[512,64]{0,1:T(8,128)} %param.11) | copy-start | bytes 393220
  2.5 18.2 %copy-start.4 = (f32[512,64]{0,1:T(8,128)S(1)}, f32[512,64]{0,1:T(8,128)}, u32[]{:S(2)}) copy-start(f32[512,64]{0,1:T(8,128)} %param.13) | copy-start | bytes 393220
  2.5 31.3 %all-to-all-start = ((bf16[256,4,128]{2,1,0:T(4,128)(2,1)}), bf16[256,4,128]{2,1,0:T(4,128)(2,1)S(1)}, u32[]{:S(2)}, u32[]{:S(2)}) async-start(bf16[256,4,128]{2,1,0:T(4,128)(2,1)} %bitcast.156), calls=%async_computation | async-start | bytes 524288 | tf_op jit(solution)/shard_map/all_to_all | solution.py:291
  18.2 2.5 %copy-start.3 = (f32[512,64]{0,1:T(8,128)S(1)}, f32[512,64]{0,1:T(8,128)}, u32[]{:S(2)}) copy-start(f32[512,64]{0,1:T(8,128)} %param.14) | copy-start | bytes 393220
  33.7 0.7 copy-start

commit v2 on v1

--- a/solution.py
+++ b/solution.py
@@ -5,13 +5,16 @@
 from jax import lax
 from jax.experimental import pallas as pl
 from jax.experimental.pallas import tpu as pltpu
+from jax.sharding import Mesh
 from jax.sharding import PartitionSpec as P
 
-AXES = ("dp", "ctx")
+OWNER = ("core", "dpair", "ctx")
+CHIP = ("dpair", "ctx")
 F32 = jnp.float32
 BF16 = jnp.bfloat16
 ROWS_IN = 4
-ROWS_OUT = 8
+ROWS_OUT = 10
+LIMIT = pltpu.CompilerParams(vmem_limit_bytes=16 * 1024 * 1024)
 FLIP = (((1,), (1,)), ((), ()))
 PLAIN = (((1,), (0,)), ((), ()))
 OUTER = (((0,), (0,)), ((), ()))
@@ -222,30 +225,41 @@
         misc,
         jnp.zeros((1, poles), F32),
     ]
-    outs[pl.ds(0, sources, stride=ROWS_OUT), :] = back[:, :span]
-    outs[pl.ds(1, sources, stride=ROWS_OUT), :] = back[:, span:]
+    chips = sources // 2
+    for core in range(2):
+        for chan in range(2):
+            outs[pl.ds(2 * core + chan, chips, stride=ROWS_OUT), :] = back[
+                core * chips : (core + 1) * chips, chan * span : (chan + 1) * span
+            ]
     for index, value in enumerate(lines):
-        outs[pl.ds(2 + index, sources, stride=ROWS_OUT), :] = jnp.broadcast_to(
-            value, (sources, poles)
-        )
+        outs[pl.ds(4 + index, chips, stride=ROWS_OUT), :] = jnp.broadcast_to(value, (chips, poles))
     out_ref[...] = outs[...].astype(BF16)
 
 
-def finish_kernel(recv_ref, grad_ref, a_ref, b_ref, c_ref, d_ref, misc_ref, rows):
-    owners = rows.shape[0] // ROWS_OUT
+def finish_kernel(core_ref, mine_ref, other_ref, grad_ref, a_ref, b_ref, c_ref, d_ref, dt_ref, skip_ref, rows):
+    chips = rows.shape[1] // ROWS_OUT
     half = a_ref.shape[0]
-    rows[...] = recv_ref[...].astype(F32)
-
-    def turned(index):
-        return rows[pl.ds(index, owners, stride=ROWS_OUT), :].T
-
-    for part in range(2):
-        grad_ref[:, part * owners : (part + 1) * owners] = turned(part).astype(BF16)
-    for index, ref in enumerate((a_ref, b_ref, c_ref, d_ref)):
-        block = turned(2 + index)
-        ref[:, :owners] = block[:half]
-        ref[:, owners:] = block[half:]
-    misc_ref[...] = turned(6)[0:8]
+    core = core_ref[0]
+    rows[core] = mine_ref[...].astype(F32)
+    rows[1 - core] = other_ref[...].astype(F32)
+
+    def turned(owner, index):
+        return rows[owner, pl.ds(index, chips, stride=ROWS_OUT), :].T
+
+    for owner in range(2):
+        for chan in range(2):
+            at = (2 * chan + owner) * chips
+            grad_ref[:, at : at + chips] = turned(owner, 2 * core + chan).astype(BF16)
+        for index, ref in enumerate((a_ref, b_ref, c_ref, d_ref)):
+            block = turned(owner, 4 + index)
+            for chan in range(2):
+                at = (2 * chan + owner) * chips
+                ref[:, at : at + chips] = block[chan * half : (chan + 1) * half]
+        misc = turned(owner, 8)
+        for chan in range(2):
+            at = (2 * chan + owner) * chips
+            dt_ref[:, at : at + chips] = misc[chan : chan + 1]
+            skip_ref[:, at : at + chips] = misc[2 + chan : 3 + chan]
 
 
 def pole_lines(step_size, pole_re, a_im, c_re, c_im):
@@ -274,12 +288,12 @@
 
 
 def body(inputs, grad_out, log_dt, log_a_re, a_im, c_re, c_im, skip_gain):
-    batch = lax.axis_size("dp")
+    batch = lax.axis_size("dpair") * lax.axis_size("core")
     devices = batch * lax.axis_size("ctx")
     span, channels = inputs.shape[1:]
     poles = a_im.shape[1]
     assert channels == 2 * devices and span == 2 * poles
-    place = lax.axis_index(AXES)
+    place = lax.axis_index(OWNER)
 
     sent = pl.pallas_call(
         send_kernel,
@@ -287,9 +301,10 @@
         in_specs=vmem(2),
         out_specs=vmem(1)[0],
         scratch_shapes=[pltpu.VMEM((devices * ROWS_IN, span), F32)],
+        compiler_params=LIMIT,
     )(inputs[0], grad_out[0])
     recv = lax.all_to_all(
-        sent.reshape(devices, ROWS_IN, span), AXES, split_axis=0, concat_axis=0, tiled=True
+        sent.reshape(devices, ROWS_IN, span), OWNER, split_axis=0, concat_axis=0, tiled=True
     ).reshape(devices * ROWS_IN, span)
 
     def own(value):
@@ -328,48 +343,53 @@
         out_shape=[tall] * 4 + [square] * 4,
         in_specs=vmem(1),
         out_specs=vmem(8),
+        compiler_params=LIMIT,
     )(cols)
     grid = pltpu.VMEM((devices, span), F32)
+    chips = devices // 2
     answer = pl.pallas_call(
         functools.partial(core_kernel, batch),
-        out_shape=jax.ShapeDtypeStruct((devices * ROWS_OUT, span), BF16),
+        out_shape=jax.ShapeDtypeStruct((chips * ROWS_OUT, span), BF16),
         in_specs=vmem(10),
         out_specs=vmem(1)[0],
         scratch_shapes=[pltpu.VMEM((devices * ROWS_IN, span), F32)]
         + [grid] * 8
-        + [pltpu.VMEM((devices * ROWS_OUT, span), F32)],
+        + [pltpu.VMEM((chips * ROWS_OUT, span), F32)],
+        compiler_params=LIMIT,
     )(recv, *tables, prm)
-    back = lax.all_to_all(
-        answer.reshape(devices, ROWS_OUT, span), AXES, split_axis=0, concat_axis=0, tiled=True
-    ).reshape(devices * ROWS_OUT, span)
+    mine = lax.all_to_all(
+        answer.reshape(chips, ROWS_OUT // 2, 2, span), CHIP, split_axis=0, concat_axis=0, tiled=True
+    ).reshape(chips * ROWS_OUT, span)
+    other = lax.ppermute(mine, "core", [(0, 1), (1, 0)])
     line = jax.ShapeDtypeStruct((poles, channels), F32)
+    single = jax.ShapeDtypeStruct((1, channels), F32)
     results = pl.pallas_call(
         finish_kernel,
-        out_shape=[jax.ShapeDtypeStruct((span, channels), BF16)]
-        + [line] * 4
-        + [jax.ShapeDtypeStruct((8, devices), F32)],
-        in_specs=vmem(1),
-        out_specs=vmem(6),
-        scratch_shapes=[pltpu.VMEM((devices * ROWS_OUT, span), F32)],
-    )(back)
-    misc = results[5]
+        out_shape=[jax.ShapeDtypeStruct((span, channels), BF16)] + [line] * 4 + [single] * 2,
+        in_specs=[pl.BlockSpec(memory_space=pltpu.SMEM)] + vmem(2),
+        out_specs=vmem(7),
+        scratch_shapes=[pltpu.VMEM((2, chips * ROWS_OUT, span), F32)],
+        compiler_params=LIMIT,
+    )(lax.axis_index("core").reshape(1), mine, other)
     return (
         results[0][None],
-        misc[0:2].reshape(channels),
+        results[5].reshape(channels),
         results[1].T,
         results[2].T,
         results[3].T,
         results[4].T,
-        misc[2:4].reshape(channels),
+        results[6].reshape(channels),
     )
 
 
 def solution(mesh):
-    placed = (P("dp", "ctx", None), P("dp", "ctx", None), P(), P(), P(), P(), P(), P())
+    pairs, ctx = mesh.devices.shape[0] // 2, mesh.devices.shape[1]
+    fine = Mesh(mesh.devices.reshape(pairs, 2, ctx), ("dpair", "core", "ctx"))
+    block = P(("dpair", "core"), "ctx", None)
     return jax.shard_map(
         body,
-        mesh=mesh,
-        in_specs=placed,
-        out_specs=(P("dp", "ctx", None), P(), P(), P(), P(), P(), P()),
+        mesh=fine,
+        in_specs=(block, block, P(), P(), P(), P(), P(), P()),
+        out_specs=(block, P(), P(), P(), P(), P(), P()),
         check_vma=False,
     )

time: 71.7 us -> 62.5 us (0.87)
  blocking collectives: 28.3 us -> 20.5 us
  Pallas kernels: 11.1 us -> 5.03 us
  waiting for transfers between devices: 6.38 us -> 11.4 us
  local copies, waits for them, and re-layouts: 7.26 us -> 4.62 us
  starting transfers between devices: 15.7 us -> 18.1 us
    all_to_all x1, blocking collectives: 28.3 us -> 20.5 us  [body(): lax.all_to_all(answer.reshape(chips, ROWS_OUT // 2, 2, span), CHIP, split...]
    all_to_all x1, waiting for transfers between devices: 6.38 us -> 10.1 us  [body(): lax.all_to_all(sent.reshape(devices, ROWS_IN, span), OWNER, split_axis=0,...]
    ppermute x0 -> x1, starting transfers between devices: none -> 2.4 us  [body(): other = lax.ppermute(mine, 'core', [(0, 1), (1, 0)])]
    pallas_call x1, Pallas kernels: 4.56 us -> 2.25 us  [body(): pl.pallas_call(functools.partial(core_kernel, batch), out_shape=jax.Shape...]
    pallas_call x1, Pallas kernels: 2.66 us -> 0.8 us  [body(): pl.pallas_call(table_kernel, out_shape=[tall] * 4 + [square] * 4, in_spec...]
    ppermute x0 -> x1, waiting for transfers between devices: none -> 1.26 us  [body(): other = lax.ppermute(mine, 'core', [(0, 1), (1, 0)])]
    another operation x3, local copies, waits for them, and re-layouts: 2.52 us -> 1.35 us  [body(): jnp.stack([far * jnp.cos(w_im * span), far * jnp.sin(w_im * span)] + list...]
    pallas_call x1, Pallas kernels: 1.82 us -> 0.86 us  [body(): pl.pallas_call(send_kernel, out_shape=jax.ShapeDtypeStruct((devices * ROW...]
  transfers between devices with their start and end apart: 1 -> 2, of which waited for: 1 -> 2; matrix products, arithmetic and copies ran while one was open for 9% -> 7% of each run, Pallas kernels for 4% -> 1%
where the time goes in v2:
time: 62.5 us; the launch traced here: 62.3 us
  blocking collectives  20.5 us (33%)
  starting transfers between devices  18.1 us (29%)
  waiting for transfers between devices  11.4 us (18%)
  Pallas kernels  5.03 us (8%)
  local copies, waits for them, and re-layouts  4.62 us (7%)
  other arithmetic  1.81 us (3%)
  between operations  0.8 us (1%)
    all_to_all x1, blocking collectives, body(): lax.all_to_all(answer.reshape(chips, ROWS_OUT // 2, 2, span), CHIP, split...  20.5 us
    all_to_all x1, starting transfers between devices, body(): lax.all_to_all(sent.reshape(devices, ROWS_IN, span), OWNER, split_axis=0,...  15.7 us
    all_to_all x1, waiting for transfers between devices, body(): lax.all_to_all(sent.reshape(devices, ROWS_IN, span), OWNER, split_axis=0,...  10.1 us
    ppermute x1, starting transfers between devices, body(): other = lax.ppermute(mine, 'core', [(0, 1), (1, 0)])  2.4 us
    pallas_call x1, Pallas kernels, body(): pl.pallas_call(functools.partial(core_kernel, batch), out_shape=jax.Shape...  2.25 us
    unnamed x16, local copies, waits for them, and re-layouts  1.83 us
    exp x1, other arithmetic, body(): step_size = jnp.exp(own_flat(log_dt))  1.37 us
    another operation x3, local copies, waits for them, and re-layouts, body(): jnp.stack([far * jnp.cos(w_im * span), far * jnp.sin(w_im * span)] + list...  1.35 us
  transfers between devices with their start and end apart: 2, of which 2 were waited for; matrix products, arithmetic and copies ran while one was open for 7% of the time, Pallas kernels for 1%

profile of v2, /device:TPU:1, one launch (start us, length us, event | category | flops | bytes accessed | tf_op | source)
XLA Modules:
  0.0 62.3 jit_solution(4581147184341071067)
XLA Ops:
  0.6 0.0 copy-start
  0.6 0.9 %copy-done = bf16[1,128,512]{2,1,0:T(8,128)(2,1)S(1)} copy-done((bf16[1,128,512]{2,1,0:T(8,128)(2,1)S(1)}, bf16[1,128,512]{2,1,0:T(8,128)(2,1)}, u32[]{:S(2)}) %copy-start) | copy-done | bytes 131096
  1.5 0.0 copy-start.1
  1.5 0.9 %copy-done.1 = bf16[1,128,512]{2,1,0:T(8,128)(2,1)S(1)} copy-done((bf16[1,128,512]{2,1,0:T(8,128)(2,1)S(1)}, bf16[1,128,512]{2,1,0:T(8,128)(2,1)}, u32[]{:S(2)}) %copy-start.1) | copy-done | bytes 131096
  2.4 0.9 %shard_map.135 = bf16[1024,128]{1,0:T(8,128)(2,1)} custom-call(bf16[128,512]{1,0:T(8,128)(2,1)S(1)} %bitcast.154, bf16[128,512]{1,0:T(8,128)(2,1)S(1)} %bitcast.155), custom_call_target="tpu_custom_call" | custom-call | tf_op jit(solution)/shard_map/pallas_call | solution.py:298
  3.3 0.0 copy-start.6
  3.3 0.0 copy-start.7
  3.3 0.0 copy-start.2
  3.3 0.0 copy-start.3
  3.3 0.0 copy-start.5
  3.3 15.7 %all-to-all-start = ((bf16[256,4,128]{2,1,0:T(4,128)(2,1)}), bf16[256,4,128]{2,1,0:T(4,128)(2,1)S(1)}, u32[]{:S(2)}, u32[]{:S(2)}) async-start(bf16[256,4,128]{2,1,0:T(4,128)(2,1)} %bitcast.3), calls=%async_computation | async-start | bytes 524288 | tf_op jit(solution)/shard_map/all_to_all | solution.py:306
  19.0 0.0 copy-start.4
  19.0 0.0 copy-done.6
  19.0 0.0 copy-done.7
  19.0 0.6 fusion.28
  19.6 1.4 %maximum_exponential_fusion = f32[2]{0:T(128)S(1)} fusion(f32[1]{0:T(128)} %get-tuple-element.82, f32[1]{0:T(128)} %get-tuple-element.83), kind=kLoop, calls=%fused_computation.13 | loop fusion | flops 2 | bytes 16 | tf_op jit(solution)/shard_map/exp | solution.py:321
  21.0 0.1 broadcast_in_dim.6
  21.1 0.1 exp.224
  21.2 0.1 exp.221
  21.2 0.0 copy-done.2
  21.3 0.0 copy-done.3
  21.3 0.2 dynamic-slice_reduce_fusion.5
  21.5 0.0 copy-done.5
  21.5 0.0 copy-done.4
  21.5 0.2 dynamic-slice_reduce_fusion.1
  21.8 0.1 negate_bitcast_fusion
  21.8 0.1 fusion.27
  22.0 0.1 fusion.17
  22.0 0.1 fusion.13
  22.1 0.1 add_divide_fusion
  22.2 0.1 copy.35.cols_ref
  22.3 0.8 %shard_map.136 = (bf16[512,256]{1,0:T(8,128)(2,1)S(1)}, bf16[512,256]{1,0:T(8,128)(2,1)S(1)}, bf16[512,256]{1,0:T(8,128)(2,1)S(1)}, bf16[512,256]{1,0:T(8,128)(2...) custom-call(f32[128,4]{1,0:T(8,128)S(1)} %copy.35.cols_ref), custom_call_target="tpu_custom_call" | custom-call | tf_op jit(solution)/shard_map/pallas_call | solution.py:341
  23.2 0.6 %stack_broadcast_in_dim.5 = f32[1,128]{1,0:T(1,128)S(1)} broadcast(f32[]{:T(128)} %bitcast.11), dimensions={} | broadcast | bytes 516 | tf_op jit(solution)/shard_map/stack;broadcast_in_dim | solution.py:331
  23.8 0.6 %stack_broadcast_in_dim.4 = f32[1,128]{1,0:T(1,128)S(1)} broadcast(f32[]{:T(128)} %bitcast.10), dimensions={} | broadcast | bytes 516 | tf_op jit(solution)/shard_map/stack;broadcast_in_dim | solution.py:331
  24.5 0.1 stack.5.prm_ref
  24.5 10.1 %all-to-all-done = bf16[256,4,128]{2,1,0:T(4,128)(2,1)S(1)} async-done(((bf16[256,4,128]{2,1,0:T(4,128)(2,1)}), bf16[256,4,128]{2,1,0:T(4,128)(2,1)S(1)}, u32[]{:S(2)}, u32[]{:S(2)}) %all-to-all-start) | async-done | bytes 262176 | tf_op jit(solution)/shard_map/all_to_all | solution.py:306
  34.7 2.2 %shard_map.137 = bf16[1280,128]{1,0:T(8,128)(2,1)S(1)} custom-call(bf16[1024,128]{1,0:T(8,128)(2,1)S(1)} %bitcast.153, bf16[512,256]{1,0:T(8,128)(2,1)S(1)} %get-tuple-element.22.fwd_hi, bf16[512,256]{1,0:T(8,128)(2,1)S(1)} %get-tuple-element.23.fwd_lo, bf16[512,256]{1,0:T(8,128)(2,1)S(1)} %get-tuple-element.24.rev_hi, ...), custom_call_target="tpu_custom_call" | custom-call | tf_op jit(solution)/shard_map/pallas_call | solution.py:350
  36.9 20.5 %all_to_all.10 = bf16[128,5,2,128]{3,2,1,0:T(2,128)(2,1)S(1)} all-to-all(bf16[128,5,2,128]{3,2,1,0:T(2,128)(2,1)S(1)} %bitcast.152), channel_id=1, replica_groups=mesh['dpair'=2,'core'=2,'ctx'=64] {'dpair','ctx'}, dimensions={0} | all-to-all | bytes 655360 | tf_op jit(solution)/shard_map/all_to_all | solution.py:360
  57.5 2.4 %collective-permute-start = (bf16[1280,128]{1,0:T(8,128)(2,1)S(1)}, bf16[1280,128]{1,0:T(8,128)(2,1)S(1)}, u32[]{:S(2)}, u32[]{:S(2)}) collective-permute-start(bf16[1280,128]{1,0:T(8,128)(2,1)S(1)} %bitcast.150), channel_id=1, source_target_pairs={{0,64},{64,0},{1,65},{65,1},{2,66},{66,2},{3,67},{67,3},{4,68},{68... | collective-permute-start | bytes 983048 | tf_op jit(solution)/shard_map/ppermute | solution.py:363
  59.9 1.3 %collective-permute-done.other_ref = bf16[1280,128]{1,0:T(8,128)(2,1)S(1)} collective-permute-done((bf16[1280,128]{1,0:T(8,128)(2,1)S(1)}, bf16[1280,128]{1,0:T(8,128)(2,1)S(1)}, u32[]{:S(2)}, u32[]{:S(2)}) %collective-permute-start) | collective-permute-done | bytes 327712 | tf_op jit(solution)/shard_map/ppermute | solution.py:363
  61.1 1.1 %shard_map.138 = (bf16[128,512]{1,0:T(8,128)(2,1)}, f32[64,512]{1,0:T(8,128)}, f32[64,512]{1,0:T(8,128)}, f32[64,512]{1,0:T(8,128)}, f32[64,512]{1,0:T(8,128)}, /*index=5*/f32[1,512]{1,0:T(1,128)}, f32[1,512]{1,0:T(1,128)}) custom-call(s32[1]{0:T(128)} %bitcast.core_ref, bf16[1280,128]{1,0:T(8,128)(2,1)S(1)} %bitcast.151, ...), custom_call_target="tpu_custom_call" | custom-call | tf_op jit(solution)/shard_map/pallas_call | solution.py:366
  (5 shorter events, 0.1 us)
Async XLA Ops:
  0.6 0.9 %copy-start = (bf16[1,128,512]{2,1,0:T(8,128)(2,1)S(1)}, bf16[1,128,512]{2,1,0:T(8,128)(2,1)}, u32[]{:S(2)}) copy-start(bf16[1,128,512]{2,1,0:T(8,128)(2,1)} %param.8) | copy-start | bytes 393220
  1.5 0.9 %copy-start.1 = (bf16[1,128,512]{2,1,0:T(8,128)(2,1)S(1)}, bf16[1,128,512]{2,1,0:T(8,128)(2,1)}, u32[]{:S(2)}) copy-start(bf16[1,128,512]{2,1,0:T(8,128)(2,1)} %param.9) | copy-start | bytes 393220
  3.3 15.7 %copy-start.6 = (f32[512]{0:T(512)S(1)}, f32[512]{0:T(512)}, u32[]{:S(2)}) copy-start(f32[512]{0:T(512)} %param.15) | copy-start | bytes 6148
  3.3 15.7 %copy-start.7 = (f32[512]{0:T(512)S(1)}, f32[512]{0:T(512)}, u32[]{:S(2)}) copy-start(f32[512]{0:T(512)} %param.10) | copy-start | bytes 6148
  3.3 17.9 %copy-start.2 = (f32[512,64]{0,1:T(8,128)S(1)}, f32[512,64]{0,1:T(8,128)}, u32[]{:S(2)}) copy-start(f32[512,64]{0,1:T(8,128)} %param.12) | copy-start | bytes 393220
  3.3 17.9 %copy-start.3 = (f32[512,64]{0,1:T(8,128)S(1)}, f32[512,64]{0,1:T(8,128)}, u32[]{:S(2)}) copy-start(f32[512,64]{0,1:T(8,128)} %param.11) | copy-start | bytes 393220
  3.3 18.2 %copy-start.5 = (f32[512,64]{0,1:T(8,128)S(1)}, f32[512,64]{0,1:T(8,128)}, u32[]{:S(2)}) copy-start(f32[512,64]{0,1:T(8,128)} %param.13) | copy-start | bytes 393220
  3.3 31.4 %all-to-all-start = ((bf16[256,4,128]{2,1,0:T(4,128)(2,1)}), bf16[256,4,128]{2,1,0:T(4,128)(2,1)S(1)}, u32[]{:S(2)}, u32[]{:S(2)}) async-start(bf16[256,4,128]{2,1,0:T(4,128)(2,1)} %bitcast.3), calls=%async_computation | async-start | bytes 524288 | tf_op jit(solution)/shard_map/all_to_all | solution.py:306
  19.0 2.5 %copy-start.4 = (f32[512,64]{0,1:T(8,128)S(1)}, f32[512,64]{0,1:T(8,128)}, u32[]{:S(2)}) copy-start(f32[512,64]{0,1:T(8,128)} %param.14) | copy-start | bytes 393220
  57.5 3.7 %collective-permute-start = (bf16[1280,128]{1,0:T(8,128)(2,1)S(1)}, bf16[1280,128]{1,0:T(8,128)(2,1)S(1)}, u32[]{:S(2)}, u32[]{:S(2)}) collective-permute-start(bf16[1280,128]{1,0:T(8,128)(2,1)S(1)} %bitcast.150), channel_id=1, source_target_pairs={{0,64},{64,0},{1,65},{65,1},{2,66},{66,2},{3,67},{67,3},{4,68},{68... | collective-permute-start | bytes 983048 | tf_op jit(solution)/shard_map/ppermute | solution.py:363

commit v3 on v2

--- a/solution.py
+++ b/solution.py
@@ -8,12 +8,14 @@
 from jax.sharding import Mesh
 from jax.sharding import PartitionSpec as P
 
-OWNER = ("core", "dpair", "ctx")
-CHIP = ("dpair", "ctx")
+OWNER = ("ctx", "dpair", "core")
+CHIP = ("ctx", "dpair")
 F32 = jnp.float32
 BF16 = jnp.bfloat16
 ROWS_IN = 4
 ROWS_OUT = 10
+SEND_PIECES = 4
+EVERY = 8
 LIMIT = pltpu.CompilerParams(vmem_limit_bytes=16 * 1024 * 1024)
 FLIP = (((1,), (1,)), ((), ()))
 PLAIN = (((1,), (0,)), ((), ()))
@@ -30,17 +32,36 @@
     return lax.dot_general(a, b, dims, preferred_element_type=F32)
 
 
-def send_kernel(inputs_ref, grad_ref, out_ref, rows):
+def send_kernel(inputs_ref, grad_ref, out_ref, stage, rows, packed, sems):
     owners = rows.shape[0] // ROWS_IN
-    for part, ref in enumerate((inputs_ref, grad_ref)):
-        block = ref[...].astype(F32)
+    chips = owners // 2
+    loads = [
+        pltpu.make_async_copy(ref, stage.at[part], sems.at[part])
+        for part, ref in enumerate((inputs_ref, grad_ref))
+    ]
+    for load in loads:
+        load.start()
+    for part, load in enumerate(loads):
+        load.wait()
         for half in range(2):
-            piece = block[:, half * owners : (half + 1) * owners].T
-            rows[pl.ds(2 * part + half, owners, stride=ROWS_IN), :] = piece
-    out_ref[...] = rows[...].astype(BF16)
-
-
-def table_kernel(cols_ref, fwd_hi, fwd_lo, rev_hi, rev_lo, mix_hi, mix_lo, band_hi, band_lo):
+            for core in range(2):
+                at = half * owners + core * chips
+                piece = stage[part, :, at : at + chips].astype(F32).T
+                line = ROWS_IN * core + 2 * part + half
+                rows[pl.ds(line, chips, stride=2 * ROWS_IN), :] = piece
+    pieces = sems.shape[0] - 2
+    size = rows.shape[0] // pieces
+    stores = []
+    for index in range(pieces):
+        at = pl.ds(index * size, size)
+        packed[at, :] = rows[at, :].astype(BF16)
+        stores.append(pltpu.make_async_copy(packed.at[at, :], out_ref.at[at, :], sems.at[2 + index]))
+        stores[-1].start()
+    for store in stores:
+        store.wait()
+
+
+def table_kernel(cols_ref, fwd_hi, fwd_lo, rev_hi, rev_lo, mix_hi, mix_lo, band_hi, band_lo, flip_ref):
     poles = cols_ref.shape[0]
     half = poles // 2
     span = poles
@@ -87,18 +108,18 @@
         hi, lo = halves(wide)
         band_hi[chan * span : (chan + 1) * span, :] = hi
         band_lo[chan * span : (chan + 1) * span, :] = lo
-
-
-def skew(value):
-    size = value.shape[0]
+    wide_sub = lax.broadcasted_iota(jnp.int32, flip_ref.shape, 0)
+    wide_lane = lax.broadcasted_iota(jnp.int32, flip_ref.shape, 1)
+    same = (wide_sub < span) == (wide_lane < span)
+    mirror = (wide_sub % span) + (wide_lane % span) == span - 1
+    flip_ref[...] = jnp.where(same & mirror, 1.0, 0.0).astype(BF16)
+
+
+def diagonals(value):
     sub = lax.broadcasted_iota(jnp.int32, value.shape, 0)
     lane = lax.broadcasted_iota(jnp.int32, value.shape, 1)
-    value = jnp.where(lane >= sub, value, 0.0)
-    bit = 1
-    while bit < size:
-        value = jnp.where((sub & bit) != 0, pltpu.roll(value, size - bit, 1), value)
-        bit *= 2
-    return value
+    value = jnp.where(lane + sub >= value.shape[0] - 1, value, 0.0)
+    return pltpu.roll(value, 1, 1, stride=1, stride_axis=0)
 
 
 def core_kernel(
@@ -112,6 +133,7 @@
     mix_lo,
     band_hi,
     band_lo,
+    flip_ref,
     prm_ref,
     out_ref,
     rows,
@@ -121,8 +143,11 @@
     d_im,
     z_re,
     z_im,
-    y_re,
-    y_im,
+    v_re,
+    v_im,
+    x_re,
+    x_im,
+    base,
     outs,
 ):
     sources = rows.shape[0] // ROWS_IN
@@ -141,53 +166,74 @@
     moments = dot(g_b, fwd_hi[...], FLIP) + dot(g_b, fwd_lo[...], FLIP)
     for index, ref in enumerate((g_re, g_im, d_re, d_im)):
         ref[...] = moments[:, index * poles : (index + 1) * poles]
+    lead = dot(u_b, rev_hi[...], FLIP) + dot(u_b, rev_lo[...], FLIP)
+    for index, ref in enumerate((v_re, v_im, x_re, x_im)):
+        ref[...] = lead[:, index * poles : (index + 1) * poles]
     prm = prm_ref[...]
 
     def line(index):
         return prm[index : index + 1, :]
 
+    def total(value):
+        return jnp.sum(value, axis=0, keepdims=True)
+
     e_re, e_im = line(0), line(1)
-    a, b, c, d = (jnp.zeros((batch, poles), F32) for _ in range(4))
+    gain = jnp.concatenate([line(14), line(15)], axis=1)
+    near = []
+    flipped = []
+    cross = []
+
+    def flip():
+        flipped.append(dot(u_b, flip_ref[...], PLAIN).astype(BF16))
+
+    def correlate():
+        cross.append(dot(flipped[0], g_b, OUTER))
+
+    def gather():
+        parts = [cross[0][k * span : (k + 1) * span, k * span : (k + 1) * span] for k in range(2)]
+        lag = jnp.concatenate([total(diagonals(value)) for value in parts], axis=1)
+        lag_hi, lag_lo = halves(jnp.broadcast_to(lag, (8, 2 * span)))
+        value = dot(lag_hi, fwd_hi[...], FLIP) + dot(lag_lo, fwd_hi[...], FLIP)
+        near.append((value + dot(lag_hi, fwd_lo[...], FLIP))[0:1])
+
+    def local(at):
+        g_rows = g_b[at : at + span]
+        value = dot(g_rows, band_hi[...], FLIP) + dot(g_rows, band_lo[...], FLIP)
+        value = value + gain * g_f[at : at + span]
+        for chan in range(2):
+            base[chan, at : at + span, :] = value[:, chan * span : (chan + 1) * span]
+
+    tasks = [flip, correlate, gather]
+    tasks += [functools.partial(local, at) for at in range(0, sources, span)]
+    a, b, c, d, s_re, s_im, t_re, t_im = (jnp.zeros((batch, poles), F32) for _ in range(8))
     for chunk in reversed(range(chunks)):
-        at = pl.ds(chunk, batch, stride=chunks)
+        at = pl.ds(chunk * batch, batch)
         z_re[at, :] = a
         z_im[at, :] = b
-        y_re[at, :] = c
-        y_im[at, :] = d
+        if chunk < chunks - 1:
+            p, q, x, y = v_re[at, :], v_im[at, :], x_re[at, :], x_im[at, :]
+            s_re, s_im = s_re + (p * a - q * b), s_im + (p * b + q * a)
+            t_re = t_re + (x * a - y * b) + (p * c - q * d)
+            t_im = t_im + (x * b + y * a) + (p * d + q * c)
         if chunk > 0:
             m = c + span * a
             n = d + span * b
             a, b = (e_re * a - e_im * b) + g_re[at, :], (e_re * b + e_im * a) + g_im[at, :]
             c, d = (e_re * m - e_im * n) + d_re[at, :], (e_re * n + e_im * m) + d_im[at, :]
-    lead = dot(u_b, rev_hi[...], FLIP) + dot(u_b, rev_lo[...], FLIP)
-    v_re, v_im = lead[:, :poles], lead[:, poles : 2 * poles]
-    x_re, x_im = lead[:, 2 * poles : 3 * poles], lead[:, 3 * poles :]
-    a, b, c, d = z_re[...], z_im[...], y_re[...], y_im[...]
-
-    def total(value):
-        return jnp.sum(value, axis=0, keepdims=True)
-
-    s_re = total(v_re * a - v_im * b)
-    s_im = total(v_re * b + v_im * a)
-    t_re = total(x_re * a - x_im * b + v_re * c - v_im * d)
-    t_im = total(x_re * b + x_im * a + v_re * d + v_im * c)
-
-    state = jnp.concatenate([a, b], axis=1)
+        if chunk % EVERY == 0 and tasks:
+            tasks.pop(0)()
+    for task in tasks:
+        task()
+    near = near[0]
+    s_re, s_im, t_re, t_im = total(s_re), total(s_im), total(t_re), total(t_im)
+
+    state = jnp.concatenate([z_re[...], z_im[...]], axis=1)
     state_hi, state_lo = halves(state)
     back = dot(state_hi, mix_hi[...], PLAIN) + dot(state_lo, mix_hi[...], PLAIN)
     back = back + dot(state_hi, mix_lo[...], PLAIN)
-    back = back + dot(g_b, band_hi[...], FLIP) + dot(g_b, band_lo[...], FLIP)
-    gain = jnp.concatenate([line(14), line(15)], axis=1)
-    back = back + gain * g_f
-
-    cross = dot(u_b, g_b, OUTER)
-    lags = [
-        total(skew(cross[k * span : (k + 1) * span, k * span : (k + 1) * span])) for k in range(2)
-    ]
-    lag = jnp.broadcast_to(jnp.concatenate(lags, axis=1), (8, 2 * span))
-    lag_hi, lag_lo = halves(lag)
-    near = dot(lag_hi, fwd_hi[...], FLIP) + dot(lag_lo, fwd_hi[...], FLIP)
-    near = (near + dot(lag_hi, fwd_lo[...], FLIP))[0:1]
+    for chan in range(2):
+        base[chan] = base[chan] + back[:, chan * span : (chan + 1) * span]
+
     s_re = s_re + near[:, :poles]
     s_im = s_im + near[:, poles : 2 * poles]
     t_re = t_re + near[:, 2 * poles : 3 * poles]
@@ -228,8 +274,8 @@
     chips = sources // 2
     for core in range(2):
         for chan in range(2):
-            outs[pl.ds(2 * core + chan, chips, stride=ROWS_OUT), :] = back[
-                core * chips : (core + 1) * chips, chan * span : (chan + 1) * span
+            outs[pl.ds(2 * core + chan, chips, stride=ROWS_OUT), :] = base[
+                chan, pl.ds(core, chips, stride=2), :
             ]
     for index, value in enumerate(lines):
         outs[pl.ds(4 + index, chips, stride=ROWS_OUT), :] = jnp.broadcast_to(value, (chips, poles))
@@ -293,15 +339,20 @@
     span, channels = inputs.shape[1:]
     poles = a_im.shape[1]
     assert channels == 2 * devices and span == 2 * poles
-    place = lax.axis_index(OWNER)
+    chips = devices // 2
+    place = lax.axis_index("core") * chips + lax.axis_index(CHIP)
 
     sent = pl.pallas_call(
         send_kernel,
         out_shape=jax.ShapeDtypeStruct((devices * ROWS_IN, span), BF16),
-        in_specs=vmem(2),
-        out_specs=vmem(1)[0],
-        scratch_shapes=[pltpu.VMEM((devices * ROWS_IN, span), F32)],
-        compiler_params=LIMIT,
+        in_specs=[pl.BlockSpec(memory_space=pltpu.HBM)] * 2,
+        out_specs=pl.BlockSpec(memory_space=pltpu.HBM),
+        scratch_shapes=[
+            pltpu.VMEM((2, span, channels), BF16),
+            pltpu.VMEM((devices * ROWS_IN, span), F32),
+            pltpu.VMEM((devices * ROWS_IN, span), BF16),
+            pltpu.SemaphoreType.DMA((2 + SEND_PIECES,)),
+        ],
     )(inputs[0], grad_out[0])
     recv = lax.all_to_all(
         sent.reshape(devices, ROWS_IN, span), OWNER, split_axis=0, concat_axis=0, tiled=True
@@ -340,20 +391,20 @@
     square = jax.ShapeDtypeStruct((wide, wide), BF16)
     tables = pl.pallas_call(
         table_kernel,
-        out_shape=[tall] * 4 + [square] * 4,
+        out_shape=[tall] * 4 + [square] * 5,
         in_specs=vmem(1),
-        out_specs=vmem(8),
+        out_specs=vmem(9),
         compiler_params=LIMIT,
     )(cols)
     grid = pltpu.VMEM((devices, span), F32)
-    chips = devices // 2
     answer = pl.pallas_call(
         functools.partial(core_kernel, batch),
         out_shape=jax.ShapeDtypeStruct((chips * ROWS_OUT, span), BF16),
-        in_specs=vmem(10),
+        in_specs=vmem(11),
         out_specs=vmem(1)[0],
         scratch_shapes=[pltpu.VMEM((devices * ROWS_IN, span), F32)]
-        + [grid] * 8
+        + [grid] * 10
+        + [pltpu.VMEM((2, devices, span), F32)]
         + [pltpu.VMEM((chips * ROWS_OUT, span), F32)],
         compiler_params=LIMIT,
     )(recv, *tables, prm)

time: 62.5 us -> 59.4 us (0.950)
  blocking collectives: 20.5 us -> 17.5 us
  local copies, waits for them, and re-layouts: 4.62 us -> 2.83 us
  starting transfers between devices: 18.1 us -> 19.3 us
    all_to_all x1, blocking collectives: 20.5 us -> 17.5 us  [body(): lax.all_to_all(answer.reshape(chips, ROWS_OUT // 2, 2, span), CHIP, split...]
    unnamed x16 -> x12, local copies, waits for them, and re-layouts: 1.83 us -> 0.04 us
    ppermute x1, starting transfers between devices: 2.4 us -> 3.63 us  [body(): other = lax.ppermute(mine, 'core', [(0, 1), (1, 0)])]
    pallas_call x1, Pallas kernels: 0.86 us -> 1.85 us  [body(): pl.pallas_call(send_kernel, out_shape=jax.ShapeDtypeStruct((devices * ROW...]
  transfers between devices with their start and end apart: 2 -> 2, of which waited for: 2 -> 2; matrix products, arithmetic and copies ran while one was open for 7% -> 8% of each run, Pallas kernels for 1% -> 1%
where the time goes in v3:
time: 59.4 us; the launch traced here: 59.2 us
  starting transfers between devices  19.3 us (32%)
  blocking collectives  17.5 us (29%)
  waiting for transfers between devices  11.3 us (19%)
  Pallas kernels  5.55 us (9%)
  local copies, waits for them, and re-layouts  2.83 us (5%)
  other arithmetic  1.81 us (3%)
  between operations  0.83 us (1%)
    all_to_all x1, blocking collectives, body(): lax.all_to_all(answer.reshape(chips, ROWS_OUT // 2, 2, span), CHIP, split...  17.5 us
    all_to_all x1, starting transfers between devices, body(): lax.all_to_all(sent.reshape(devices, ROWS_IN, span), OWNER, split_axis=0,...  15.7 us
    all_to_all x1, waiting for transfers between devices, body(): lax.all_to_all(sent.reshape(devices, ROWS_IN, span), OWNER, split_axis=0,...  10.1 us
    ppermute x1, starting transfers between devices, body(): other = lax.ppermute(mine, 'core', [(0, 1), (1, 0)])  3.63 us
    pallas_call x1, Pallas kernels, body(): pl.pallas_call(send_kernel, out_shape=jax.ShapeDtypeStruct((devices * ROW...  1.85 us
    pallas_call x1, Pallas kernels, body(): pl.pallas_call(functools.partial(core_kernel, batch), out_shape=jax.Shape...  1.78 us
    exp x1, other arithmetic, body(): step_size = jnp.exp(own_flat(log_dt))  1.37 us
    another operation x3, local copies, waits for them, and re-layouts, body(): jnp.stack([far * jnp.cos(w_im * span), far * jnp.sin(w_im * span)] + list...  1.35 us
  transfers between devices with their start and end apart: 2, of which 2 were waited for; matrix products, arithmetic and copies ran while one was open for 8% of the time, Pallas kernels for 1%

profile of v3, /device:TPU:1, one launch (start us, length us, event | category | flops | bytes accessed | tf_op | source)
XLA Modules:
  0.0 59.2 jit_solution(6533624106536099395)
XLA Ops:
  0.6 1.8 %shard_map.135 = bf16[1024,128]{1,0:T(8,128)(2,1)} custom-call(bf16[128,512]{1,0:T(8,128)(2,1)} %bitcast.155, bf16[128,512]{1,0:T(8,128)(2,1)} %bitcast.156), custom_call_target="tpu_custom_call" | custom-call | tf_op jit(solution)/shard_map/pallas_call | solution.py:345
  2.5 0.0 copy-start.4
  2.5 0.0 copy-start.5
  2.5 0.0 copy-start
  2.5 0.0 copy-start.1
  2.5 0.0 copy-start.3
  2.5 15.7 %all-to-all-start = ((bf16[256,4,128]{2,1,0:T(4,128)(2,1)}), bf16[256,4,128]{2,1,0:T(4,128)(2,1)S(1)}, u32[]{:S(2)}, u32[]{:S(2)}) async-start(bf16[256,4,128]{2,1,0:T(4,128)(2,1)} %bitcast.154), calls=%async_computation | async-start | bytes 524288 | tf_op jit(solution)/shard_map/all_to_all | solution.py:357
  18.2 0.0 copy-start.2
  18.2 0.0 copy-done.4
  18.3 0.0 copy-done.5
  18.3 0.6 %fusion.28 = (f32[1]{0:T(128)}, f32[1]{0:T(128)}, f32[1]{0:T(128)}, f32[1]{0:T(128)}) fusion(f32[512]{0:T(512)S(1)} %copy-done.4, s32[]{:T(128)S(6)} %select_n.5, s32[]{:T(128)S(6)} %select_n.4, f32[512]{0:T(512)S(1)} %copy-done.5), kind=kLoop, calls=%fused_computation.70 | loop fusion | bytes 40 | tf_op jit(solution)/shard_map/dynamic_slice | solution.py:379
  18.9 1.4 %maximum_exponential_fusion = f32[2]{0:T(128)S(1)} fusion(f32[1]{0:T(128)} %get-tuple-element.84, f32[1]{0:T(128)} %get-tuple-element.85), kind=kLoop, calls=%fused_computation.13 | loop fusion | flops 2 | bytes 16 | tf_op jit(solution)/shard_map/exp | solution.py:372
  20.2 0.1 broadcast_in_dim.6
  20.3 0.1 exp.224
  20.4 0.1 exp.221
  20.5 0.0 copy-done
  20.5 0.0 copy-done.1
  20.5 0.2 dynamic-slice_reduce_fusion.5
  20.7 0.0 copy-done.3
  20.7 0.0 copy-done.2
  20.7 0.2 dynamic-slice_reduce_fusion.1
  21.0 0.1 negate_bitcast_fusion
  21.1 0.1 fusion.27
  21.2 0.1 fusion.17
  21.3 0.1 fusion.13
  21.4 0.1 add_divide_fusion
  21.4 0.1 copy.35.cols_ref
  21.6 0.8 %shard_map.136 = (bf16[512,256]{1,0:T(8,128)(2,1)S(1)}, bf16[512,256]{1,0:T(8,128)(2,1)S(1)}, bf16[512,256]{1,0:T(8,128)(2,1)S(1)}, bf16[512,256]{1,0:T(8,128)(2...) custom-call(f32[128,4]{1,0:T(8,128)S(1)} %copy.35.cols_ref), custom_call_target="tpu_custom_call" | custom-call | tf_op jit(solution)/shard_map/pallas_call | solution.py:392
  22.4 0.6 %stack_broadcast_in_dim.5 = f32[1,128]{1,0:T(1,128)S(1)} broadcast(f32[]{:T(128)} %bitcast.11), dimensions={} | broadcast | bytes 516 | tf_op jit(solution)/shard_map/stack;broadcast_in_dim | solution.py:382
  23.1 0.6 %stack_broadcast_in_dim.4 = f32[1,128]{1,0:T(1,128)S(1)} broadcast(f32[]{:T(128)} %bitcast.10), dimensions={} | broadcast | bytes 516 | tf_op jit(solution)/shard_map/stack;broadcast_in_dim | solution.py:382
  23.7 0.1 stack.5.prm_ref
  23.8 10.1 %all-to-all-done = bf16[256,4,128]{2,1,0:T(4,128)(2,1)S(1)} async-done(((bf16[256,4,128]{2,1,0:T(4,128)(2,1)}), bf16[256,4,128]{2,1,0:T(4,128)(2,1)S(1)}, u32[]{:S(2)}, u32[]{:S(2)}) %all-to-all-start) | async-done | bytes 262176 | tf_op jit(solution)/shard_map/all_to_all | solution.py:357
  33.8 1.8 %shard_map.137 = bf16[1280,128]{1,0:T(8,128)(2,1)S(1)} custom-call(bf16[1024,128]{1,0:T(8,128)(2,1)S(1)} %bitcast.153, bf16[512,256]{1,0:T(8,128)(2,1)S(1)} %get-tuple-element.23.fwd_hi, bf16[512,256]{1,0:T(8,128)(2,1)S(1)} %get-tuple-element.24.fwd_lo, bf16[512,256]{1,0:T(8,128)(2,1)S(1)} %get-tuple-element.25.rev_hi, ...), custom_call_target="tpu_custom_call" | custom-call | tf_op jit(solution)/shard_map/pallas_call | solution.py:400
  35.6 17.5 %all_to_all.10 = bf16[128,5,2,128]{3,2,1,0:T(2,128)(2,1)S(1)} all-to-all(bf16[128,5,2,128]{3,2,1,0:T(2,128)(2,1)S(1)} %bitcast.150), channel_id=1, replica_groups=mesh['dpair'=2,'core'=2,'ctx'=64] {'ctx','dpair'}, dimensions={0} | all-to-all | bytes 655360 | tf_op jit(solution)/shard_map/all_to_all | solution.py:411
  53.1 3.6 %collective-permute-start = (bf16[1280,128]{1,0:T(8,128)(2,1)S(1)}, bf16[1280,128]{1,0:T(8,128)(2,1)S(1)}, u32[]{:S(2)}, u32[]{:S(2)}) collective-permute-start(bf16[1280,128]{1,0:T(8,128)(2,1)S(1)} %bitcast.151), channel_id=1, source_target_pairs={{0,64},{64,0},{1,65},{65,1},{2,66},{66,2},{3,67},{67,3},{4,68},{68... | collective-permute-start | bytes 983048 | tf_op jit(solution)/shard_map/ppermute | solution.py:414
  56.8 1.3 %collective-permute-done.other_ref = bf16[1280,128]{1,0:T(8,128)(2,1)S(1)} collective-permute-done((bf16[1280,128]{1,0:T(8,128)(2,1)S(1)}, bf16[1280,128]{1,0:T(8,128)(2,1)S(1)}, u32[]{:S(2)}, u32[]{:S(2)}) %collective-permute-start) | collective-permute-done | bytes 327712 | tf_op jit(solution)/shard_map/ppermute | solution.py:414
  58.0 1.1 %shard_map.138 = (bf16[128,512]{1,0:T(8,128)(2,1)}, f32[64,512]{1,0:T(8,128)}, f32[64,512]{1,0:T(8,128)}, f32[64,512]{1,0:T(8,128)}, f32[64,512]{1,0:T(8,128)}, /*index=5*/f32[1,512]{1,0:T(1,128)}, f32[1,512]{1,0:T(1,128)}) custom-call(s32[1]{0:T(128)} %bitcast.core_ref, bf16[1280,128]{1,0:T(8,128)(2,1)S(1)} %bitcast.152, ...), custom_call_target="tpu_custom_call" | custom-call | tf_op jit(solution)/shard_map/pallas_call | solution.py:417
  (5 shorter events, 0.1 us)
Async XLA Ops:
  2.5 15.8 %copy-start.4 = (f32[512]{0:T(512)S(1)}, f32[512]{0:T(512)}, u32[]{:S(2)}) copy-start(f32[512]{0:T(512)} %param.15) | copy-start | bytes 6148
  2.5 15.8 %copy-start.5 = (f32[512]{0:T(512)S(1)}, f32[512]{0:T(512)}, u32[]{:S(2)}) copy-start(f32[512]{0:T(512)} %param.10) | copy-start | bytes 6148
  2.5 18.0 %copy-start = (f32[512,64]{0,1:T(8,128)S(1)}, f32[512,64]{0,1:T(8,128)}, u32[]{:S(2)}) copy-start(f32[512,64]{0,1:T(8,128)} %param.12) | copy-start | bytes 393220
  2.5 18.0 %copy-start.1 = (f32[512,64]{0,1:T(8,128)S(1)}, f32[512,64]{0,1:T(8,128)}, u32[]{:S(2)}) copy-start(f32[512,64]{0,1:T(8,128)} %param.11) | copy-start | bytes 393220
  2.5 18.2 %copy-start.3 = (f32[512,64]{0,1:T(8,128)S(1)}, f32[512,64]{0,1:T(8,128)}, u32[]{:S(2)}) copy-start(f32[512,64]{0,1:T(8,128)} %param.13) | copy-start | bytes 393220
  2.5 31.3 %all-to-all-start = ((bf16[256,4,128]{2,1,0:T(4,128)(2,1)}), bf16[256,4,128]{2,1,0:T(4,128)(2,1)S(1)}, u32[]{:S(2)}, u32[]{:S(2)}) async-start(bf16[256,4,128]{2,1,0:T(4,128)(2,1)} %bitcast.154), calls=%async_computation | async-start | bytes 524288 | tf_op jit(solution)/shard_map/all_to_all | solution.py:357
  18.2 2.5 %copy-start.2 = (f32[512,64]{0,1:T(8,128)S(1)}, f32[512,64]{0,1:T(8,128)}, u32[]{:S(2)}) copy-start(f32[512,64]{0,1:T(8,128)} %param.14) | copy-start | bytes 393220
  53.1 4.9 %collective-permute-start = (bf16[1280,128]{1,0:T(8,128)(2,1)S(1)}, bf16[1280,128]{1,0:T(8,128)(2,1)S(1)}, u32[]{:S(2)}, u32[]{:S(2)}) collective-permute-start(bf16[1280,128]{1,0:T(8,128)(2,1)S(1)} %bitcast.151), channel_id=1, source_target_pairs={{0,64},{64,0},{1,65},{65,1},{2,66},{66,2},{3,67},{67,3},{4,68},{68... | collective-permute-start | bytes 983048 | tf_op jit(solution)/shard_map/ppermute | solution.py:414

commit v4 on v3

--- a/solution.py
+++ b/solution.py
@@ -15,7 +15,7 @@
 ROWS_IN = 4
 ROWS_OUT = 10
 SEND_PIECES = 4
-EVERY = 8
+SPARE = 8
 LIMIT = pltpu.CompilerParams(vmem_limit_bytes=16 * 1024 * 1024)
 FLIP = (((1,), (1,)), ((), ()))
 PLAIN = (((1,), (0,)), ((), ()))
@@ -33,7 +33,7 @@
 
 
 def send_kernel(inputs_ref, grad_ref, out_ref, stage, rows, packed, sems):
-    owners = rows.shape[0] // ROWS_IN
+    owners = packed.shape[0] // ROWS_IN
     chips = owners // 2
     loads = [
         pltpu.make_async_copy(ref, stage.at[part], sems.at[part])
@@ -50,7 +50,7 @@
                 line = ROWS_IN * core + 2 * part + half
                 rows[pl.ds(line, chips, stride=2 * ROWS_IN), :] = piece
     pieces = sems.shape[0] - 2
-    size = rows.shape[0] // pieces
+    size = packed.shape[0] // pieces
     stores = []
     for index in range(pieces):
         at = pl.ds(index * size, size)
@@ -150,12 +150,12 @@
     base,
     outs,
 ):
-    sources = rows.shape[0] // ROWS_IN
+    sources = recv_ref.shape[0] // ROWS_IN
     chunks = sources // batch
     poles = prm_ref.shape[1]
     span = poles
     half = poles // 2
-    rows[...] = recv_ref[...].astype(F32)
+    rows[: sources * ROWS_IN, :] = recv_ref[...].astype(F32)
 
     def part(index):
         return rows[pl.ds(index, sources, stride=ROWS_IN), :]
@@ -163,48 +163,31 @@
     u_f = jnp.concatenate([part(0), part(1)], axis=1)
     g_f = jnp.concatenate([part(2), part(3)], axis=1)
     u_b, g_b = u_f.astype(BF16), g_f.astype(BF16)
-    moments = dot(g_b, fwd_hi[...], FLIP) + dot(g_b, fwd_lo[...], FLIP)
-    for index, ref in enumerate((g_re, g_im, d_re, d_im)):
-        ref[...] = moments[:, index * poles : (index + 1) * poles]
+    prm = prm_ref[...]
+
+    def line(index):
+        return prm[index : index + 1, :]
+
+    def total(value):
+        return jnp.sum(value, axis=0, keepdims=True)
+
+    mirrored = dot(flip_ref[...], u_b, FLIP).astype(BF16)
+    cross = dot(mirrored, g_b, PLAIN)
     lead = dot(u_b, rev_hi[...], FLIP) + dot(u_b, rev_lo[...], FLIP)
     for index, ref in enumerate((v_re, v_im, x_re, x_im)):
-        ref[...] = lead[:, index * poles : (index + 1) * poles]
-    prm = prm_ref[...]
-
-    def line(index):
-        return prm[index : index + 1, :]
-
-    def total(value):
-        return jnp.sum(value, axis=0, keepdims=True)
-
+        ref[:sources, :] = lead[:, index * poles : (index + 1) * poles]
+    near_back = dot(g_b, band_hi[...], FLIP) + dot(g_b, band_lo[...], FLIP)
+    near_back = near_back + jnp.concatenate([line(14), line(15)], axis=1) * g_f
+    blocks = [cross[k * span : (k + 1) * span, k * span : (k + 1) * span] for k in range(2)]
+    lag = jnp.concatenate([total(diagonals(value)) for value in blocks], axis=1)
+    lag_hi, lag_lo = halves(jnp.broadcast_to(lag, (16, 2 * span)))
+    stacked = jnp.concatenate([g_b, lag_hi, lag_lo], axis=0)
+    moments = dot(stacked, fwd_hi[...], FLIP) + dot(stacked, fwd_lo[...], FLIP)
+    near = moments[sources : sources + 1] + moments[sources + 16 : sources + 17]
+    moments = moments[:sources]
+    for index, ref in enumerate((g_re, g_im, d_re, d_im)):
+        ref[:sources, :] = moments[:, index * poles : (index + 1) * poles]
     e_re, e_im = line(0), line(1)
-    gain = jnp.concatenate([line(14), line(15)], axis=1)
-    near = []
-    flipped = []
-    cross = []
-
-    def flip():
-        flipped.append(dot(u_b, flip_ref[...], PLAIN).astype(BF16))
-
-    def correlate():
-        cross.append(dot(flipped[0], g_b, OUTER))
-
-    def gather():
-        parts = [cross[0][k * span : (k + 1) * span, k * span : (k + 1) * span] for k in range(2)]
-        lag = jnp.concatenate([total(diagonals(value)) for value in parts], axis=1)
-        lag_hi, lag_lo = halves(jnp.broadcast_to(lag, (8, 2 * span)))
-        value = dot(lag_hi, fwd_hi[...], FLIP) + dot(lag_lo, fwd_hi[...], FLIP)
-        near.append((value + dot(lag_hi, fwd_lo[...], FLIP))[0:1])
-
-    def local(at):
-        g_rows = g_b[at : at + span]
-        value = dot(g_rows, band_hi[...], FLIP) + dot(g_rows, band_lo[...], FLIP)
-        value = value + gain * g_f[at : at + span]
-        for chan in range(2):
-            base[chan, at : at + span, :] = value[:, chan * span : (chan + 1) * span]
-
-    tasks = [flip, correlate, gather]
-    tasks += [functools.partial(local, at) for at in range(0, sources, span)]
     a, b, c, d, s_re, s_im, t_re, t_im = (jnp.zeros((batch, poles), F32) for _ in range(8))
     for chunk in reversed(range(chunks)):
         at = pl.ds(chunk * batch, batch)
@@ -220,19 +203,15 @@
             n = d + span * b
             a, b = (e_re * a - e_im * b) + g_re[at, :], (e_re * b + e_im * a) + g_im[at, :]
             c, d = (e_re * m - e_im * n) + d_re[at, :], (e_re * n + e_im * m) + d_im[at, :]
-        if chunk % EVERY == 0 and tasks:
-            tasks.pop(0)()
-    for task in tasks:
-        task()
-    near = near[0]
     s_re, s_im, t_re, t_im = total(s_re), total(s_im), total(t_re), total(t_im)
 
-    state = jnp.concatenate([z_re[...], z_im[...]], axis=1)
+    state = jnp.concatenate([z_re[:sources, :], z_im[:sources, :]], axis=1)
     state_hi, state_lo = halves(state)
     back = dot(state_hi, mix_hi[...], PLAIN) + dot(state_lo, mix_hi[...], PLAIN)
     back = back + dot(state_hi, mix_lo[...], PLAIN)
+    back = back + near_back
     for chan in range(2):
-        base[chan] = base[chan] + back[:, chan * span : (chan + 1) * span]
+        base[chan, :sources, :] = back[:, chan * span : (chan + 1) * span]
 
     s_re = s_re + near[:, :poles]
     s_im = s_im + near[:, poles : 2 * poles]
@@ -279,15 +258,16 @@
             ]
     for index, value in enumerate(lines):
         outs[pl.ds(4 + index, chips, stride=ROWS_OUT), :] = jnp.broadcast_to(value, (chips, poles))
-    out_ref[...] = outs[...].astype(BF16)
+    out_ref[...] = outs[: chips * ROWS_OUT, :].astype(BF16)
 
 
 def finish_kernel(core_ref, mine_ref, other_ref, grad_ref, a_ref, b_ref, c_ref, d_ref, dt_ref, skip_ref, rows):
-    chips = rows.shape[1] // ROWS_OUT
+    used = mine_ref.shape[0]
+    chips = used // ROWS_OUT
     half = a_ref.shape[0]
     core = core_ref[0]
-    rows[core] = mine_ref[...].astype(F32)
-    rows[1 - core] = other_ref[...].astype(F32)
+    rows[core, :used, :] = mine_ref[...].astype(F32)
+    rows[1 - core, :used, :] = other_ref[...].astype(F32)
 
     def turned(owner, index):
         return rows[owner, pl.ds(index, chips, stride=ROWS_OUT), :].T
@@ -349,7 +329,7 @@
         out_specs=pl.BlockSpec(memory_space=pltpu.HBM),
         scratch_shapes=[
             pltpu.VMEM((2, span, channels), BF16),
-            pltpu.VMEM((devices * ROWS_IN, span), F32),
+            pltpu.VMEM(((devices + 2 * SPARE) * ROWS_IN, span), F32),
             pltpu.VMEM((devices * ROWS_IN, span), BF16),
             pltpu.SemaphoreType.DMA((2 + SEND_PIECES,)),
         ],
@@ -396,16 +376,16 @@
         out_specs=vmem(9),
         compiler_params=LIMIT,
     )(cols)
-    grid = pltpu.VMEM((devices, span), F32)
+    grid = pltpu.VMEM((devices + SPARE, span), F32)
     answer = pl.pallas_call(
         functools.partial(core_kernel, batch),
         out_shape=jax.ShapeDtypeStruct((chips * ROWS_OUT, span), BF16),
         in_specs=vmem(11),
         out_specs=vmem(1)[0],
-        scratch_shapes=[pltpu.VMEM((devices * ROWS_IN, span), F32)]
+        scratch_shapes=[pltpu.VMEM(((devices + SPARE) * ROWS_IN, span), F32)]
         + [grid] * 10
-        + [pltpu.VMEM((2, devices, span), F32)]
-        + [pltpu.VMEM((chips * ROWS_OUT, span), F32)],
+        + [pltpu.VMEM((2, devices + 2 * SPARE, span), F32)]
+        + [pltpu.VMEM(((chips + SPARE) * ROWS_OUT, span), F32)],
         compiler_params=LIMIT,
     )(recv, *tables, prm)
     mine = lax.all_to_all(
@@ -419,7 +399,7 @@
         out_shape=[jax.ShapeDtypeStruct((span, channels), BF16)] + [line] * 4 + [single] * 2,
         in_specs=[pl.BlockSpec(memory_space=pltpu.SMEM)] + vmem(2),
         out_specs=vmem(7),
-        scratch_shapes=[pltpu.VMEM((2, chips * ROWS_OUT, span), F32)],
+        scratch_shapes=[pltpu.VMEM((2, (chips + SPARE) * ROWS_OUT, span), F32)],
         compiler_params=LIMIT,
     )(lax.axis_index("core").reshape(1), mine, other)
     return (

time: 59.4 us -> 59.1 us (level)
  no operation moved by 1% of the time
where the time goes in v4:
time: 59.1 us; the launch traced here: 58.9 us
  starting transfers between devices  19.3 us (33%)
  blocking collectives  17.5 us (30%)
  waiting for transfers between devices  11.3 us (19%)
  Pallas kernels  5.27 us (9%)
  local copies, waits for them, and re-layouts  2.83 us (5%)
  other arithmetic  1.81 us (3%)
  between operations  0.83 us (1%)
    all_to_all x1, blocking collectives, body(): lax.all_to_all(answer.reshape(chips, ROWS_OUT // 2, 2, span), CHIP, split...  17.5 us
    all_to_all x1, starting transfers between devices, body(): lax.all_to_all(sent.reshape(devices, ROWS_IN, span), OWNER, split_axis=0,...  15.7 us
    all_to_all x1, waiting for transfers between devices, body(): lax.all_to_all(sent.reshape(devices, ROWS_IN, span), OWNER, split_axis=0,...  10.1 us
    ppermute x1, starting transfers between devices, body(): other = lax.ppermute(mine, 'core', [(0, 1), (1, 0)])  3.64 us
    pallas_call x1, Pallas kernels, body(): pl.pallas_call(send_kernel, out_shape=jax.ShapeDtypeStruct((devices * ROW...  1.85 us
    pallas_call x1, Pallas kernels, body(): pl.pallas_call(functools.partial(core_kernel, batch), out_shape=jax.Shape...  1.49 us
    exp x1, other arithmetic, body(): step_size = jnp.exp(own_flat(log_dt))  1.37 us
    another operation x3, local copies, waits for them, and re-layouts, body(): jnp.stack([far * jnp.cos(w_im * span), far * jnp.sin(w_im * span)] + list...  1.35 us
  transfers between devices with their start and end apart: 2, of which 2 were waited for; matrix products, arithmetic and copies ran while one was open for 8% of the time, Pallas kernels for 1%

profile of v4, /device:TPU:1, one launch (start us, length us, event | category | flops | bytes accessed | tf_op | source)
XLA Modules:
  0.0 58.9 jit_solution(13026695005895577793)
XLA Ops:
  0.6 1.8 %shard_map.135 = bf16[1024,128]{1,0:T(8,128)(2,1)} custom-call(bf16[128,512]{1,0:T(8,128)(2,1)} %bitcast.155, bf16[128,512]{1,0:T(8,128)(2,1)} %bitcast.156), custom_call_target="tpu_custom_call" | custom-call | tf_op jit(solution)/shard_map/pallas_call | solution.py:325
  2.5 0.0 copy-start.4
  2.5 0.0 copy-start.5
  2.5 0.0 copy-start
  2.5 0.0 copy-start.1
  2.5 0.0 copy-start.3
  2.5 15.7 %all-to-all-start = ((bf16[256,4,128]{2,1,0:T(4,128)(2,1)}), bf16[256,4,128]{2,1,0:T(4,128)(2,1)S(1)}, u32[]{:S(2)}, u32[]{:S(2)}) async-start(bf16[256,4,128]{2,1,0:T(4,128)(2,1)} %bitcast.154), calls=%async_computation | async-start | bytes 524288 | tf_op jit(solution)/shard_map/all_to_all | solution.py:337
  18.2 0.0 copy-start.2
  18.2 0.0 copy-done.4
  18.3 0.0 copy-done.5
  18.3 0.6 %fusion.28 = (f32[1]{0:T(128)}, f32[1]{0:T(128)}, f32[1]{0:T(128)}, f32[1]{0:T(128)}) fusion(f32[512]{0:T(512)S(1)} %copy-done.4, s32[]{:T(128)S(6)} %select_n.5, s32[]{:T(128)S(6)} %select_n.4, f32[512]{0:T(512)S(1)} %copy-done.5), kind=kLoop, calls=%fused_computation.70 | loop fusion | bytes 40 | tf_op jit(solution)/shard_map/dynamic_slice | solution.py:359
  18.9 1.4 %maximum_exponential_fusion = f32[2]{0:T(128)S(1)} fusion(f32[1]{0:T(128)} %get-tuple-element.84, f32[1]{0:T(128)} %get-tuple-element.85), kind=kLoop, calls=%fused_computation.13 | loop fusion | flops 2 | bytes 16 | tf_op jit(solution)/shard_map/exp | solution.py:352
  20.2 0.1 broadcast_in_dim.6
  20.3 0.1 exp.224
  20.4 0.1 exp.221
  20.5 0.0 copy-done
  20.5 0.0 copy-done.1
  20.5 0.2 dynamic-slice_reduce_fusion.5
  20.7 0.0 copy-done.3
  20.7 0.0 copy-done.2
  20.7 0.2 dynamic-slice_reduce_fusion.1
  21.0 0.1 negate_bitcast_fusion
  21.1 0.1 fusion.27
  21.2 0.1 fusion.17
  21.3 0.1 fusion.13
  21.4 0.1 add_divide_fusion
  21.4 0.1 copy.35.cols_ref
  21.6 0.8 %shard_map.136 = (bf16[512,256]{1,0:T(8,128)(2,1)S(1)}, bf16[512,256]{1,0:T(8,128)(2,1)S(1)}, bf16[512,256]{1,0:T(8,128)(2,1)S(1)}, bf16[512,256]{1,0:T(8,128)(2...) custom-call(f32[128,4]{1,0:T(8,128)S(1)} %copy.35.cols_ref), custom_call_target="tpu_custom_call" | custom-call | tf_op jit(solution)/shard_map/pallas_call | solution.py:372
  22.4 0.6 %stack_broadcast_in_dim.5 = f32[1,128]{1,0:T(1,128)S(1)} broadcast(f32[]{:T(128)} %bitcast.11), dimensions={} | broadcast | bytes 516 | tf_op jit(solution)/shard_map/stack;broadcast_in_dim | solution.py:362
  23.1 0.6 %stack_broadcast_in_dim.4 = f32[1,128]{1,0:T(1,128)S(1)} broadcast(f32[]{:T(128)} %bitcast.10), dimensions={} | broadcast | bytes 516 | tf_op jit(solution)/shard_map/stack;broadcast_in_dim | solution.py:362
  23.7 0.1 stack.5.prm_ref
  23.8 10.1 %all-to-all-done = bf16[256,4,128]{2,1,0:T(4,128)(2,1)S(1)} async-done(((bf16[256,4,128]{2,1,0:T(4,128)(2,1)}), bf16[256,4,128]{2,1,0:T(4,128)(2,1)S(1)}, u32[]{:S(2)}, u32[]{:S(2)}) %all-to-all-start) | async-done | bytes 262176 | tf_op jit(solution)/shard_map/all_to_all | solution.py:337
  33.8 1.5 %shard_map.137 = bf16[1280,128]{1,0:T(8,128)(2,1)S(1)} custom-call(bf16[1024,128]{1,0:T(8,128)(2,1)S(1)} %bitcast.153, bf16[512,256]{1,0:T(8,128)(2,1)S(1)} %get-tuple-element.23.fwd_hi, bf16[512,256]{1,0:T(8,128)(2,1)S(1)} %get-tuple-element.24.fwd_lo, bf16[512,256]{1,0:T(8,128)(2,1)S(1)} %get-tuple-element.25.rev_hi, ...), custom_call_target="tpu_custom_call" | custom-call | tf_op jit(solution)/shard_map/pallas_call | solution.py:380
  35.3 17.5 %all_to_all.10 = bf16[128,5,2,128]{3,2,1,0:T(2,128)(2,1)S(1)} all-to-all(bf16[128,5,2,128]{3,2,1,0:T(2,128)(2,1)S(1)} %bitcast.150), channel_id=1, replica_groups=mesh['dpair'=2,'core'=2,'ctx'=64] {'ctx','dpair'}, dimensions={0} | all-to-all | bytes 655360 | tf_op jit(solution)/shard_map/all_to_all | solution.py:391
  52.8 3.6 %collective-permute-start = (bf16[1280,128]{1,0:T(8,128)(2,1)S(1)}, bf16[1280,128]{1,0:T(8,128)(2,1)S(1)}, u32[]{:S(2)}, u32[]{:S(2)}) collective-permute-start(bf16[1280,128]{1,0:T(8,128)(2,1)S(1)} %bitcast.151), channel_id=1, source_target_pairs={{0,64},{64,0},{1,65},{65,1},{2,66},{66,2},{3,67},{67,3},{4,68},{68... | collective-permute-start | bytes 983048 | tf_op jit(solution)/shard_map/ppermute | solution.py:394
  56.5 1.3 %collective-permute-done.other_ref = bf16[1280,128]{1,0:T(8,128)(2,1)S(1)} collective-permute-done((bf16[1280,128]{1,0:T(8,128)(2,1)S(1)}, bf16[1280,128]{1,0:T(8,128)(2,1)S(1)}, u32[]{:S(2)}, u32[]{:S(2)}) %collective-permute-start) | collective-permute-done | bytes 327712 | tf_op jit(solution)/shard_map/ppermute | solution.py:394
  57.7 1.1 %shard_map.138 = (bf16[128,512]{1,0:T(8,128)(2,1)}, f32[64,512]{1,0:T(8,128)}, f32[64,512]{1,0:T(8,128)}, f32[64,512]{1,0:T(8,128)}, f32[64,512]{1,0:T(8,128)}, /*index=5*/f32[1,512]{1,0:T(1,128)}, f32[1,512]{1,0:T(1,128)}) custom-call(s32[1]{0:T(128)} %bitcast.core_ref, bf16[1280,128]{1,0:T(8,128)(2,1)S(1)} %bitcast.152, ...), custom_call_target="tpu_custom_call" | custom-call | tf_op jit(solution)/shard_map/pallas_call | solution.py:397
  (5 shorter events, 0.1 us)
Async XLA Ops:
  2.5 15.8 %copy-start.4 = (f32[512]{0:T(512)S(1)}, f32[512]{0:T(512)}, u32[]{:S(2)}) copy-start(f32[512]{0:T(512)} %param.15) | copy-start | bytes 6148
  2.5 15.8 %copy-start.5 = (f32[512]{0:T(512)S(1)}, f32[512]{0:T(512)}, u32[]{:S(2)}) copy-start(f32[512]{0:T(512)} %param.10) | copy-start | bytes 6148
  2.5 18.0 %copy-start = (f32[512,64]{0,1:T(8,128)S(1)}, f32[512,64]{0,1:T(8,128)}, u32[]{:S(2)}) copy-start(f32[512,64]{0,1:T(8,128)} %param.12) | copy-start | bytes 393220
  2.5 18.0 %copy-start.1 = (f32[512,64]{0,1:T(8,128)S(1)}, f32[512,64]{0,1:T(8,128)}, u32[]{:S(2)}) copy-start(f32[512,64]{0,1:T(8,128)} %param.11) | copy-start | bytes 393220
  2.5 18.2 %copy-start.3 = (f32[512,64]{0,1:T(8,128)S(1)}, f32[512,64]{0,1:T(8,128)}, u32[]{:S(2)}) copy-start(f32[512,64]{0,1:T(8,128)} %param.13) | copy-start | bytes 393220
  2.5 31.3 %all-to-all-start = ((bf16[256,4,128]{2,1,0:T(4,128)(2,1)}), bf16[256,4,128]{2,1,0:T(4,128)(2,1)S(1)}, u32[]{:S(2)}, u32[]{:S(2)}) async-start(bf16[256,4,128]{2,1,0:T(4,128)(2,1)} %bitcast.154), calls=%async_computation | async-start | bytes 524288 | tf_op jit(solution)/shard_map/all_to_all | solution.py:337
  18.2 2.5 %copy-start.2 = (f32[512,64]{0,1:T(8,128)S(1)}, f32[512,64]{0,1:T(8,128)}, u32[]{:S(2)}) copy-start(f32[512,64]{0,1:T(8,128)} %param.14) | copy-start | bytes 393220
  52.8 4.9 %collective-permute-start = (bf16[1280,128]{1,0:T(8,128)(2,1)S(1)}, bf16[1280,128]{1,0:T(8,128)(2,1)S(1)}, u32[]{:S(2)}, u32[]{:S(2)}) collective-permute-start(bf16[1280,128]{1,0:T(8,128)(2,1)S(1)} %bitcast.151), channel_id=1, source_target_pairs={{0,64},{64,0},{1,65},{65,1},{2,66},{66,2},{3,67},{67,3},{4,68},{68... | collective-permute-start | bytes 983048 | tf_op jit(solution)/shard_map/ppermute | solution.py:394

commit v5 on v4

--- a/solution.py
+++ b/solution.py
@@ -1,4 +1,5 @@
 import functools
+import math
 
 import jax
 import jax.numpy as jnp
@@ -16,6 +17,7 @@
 ROWS_OUT = 10
 SEND_PIECES = 4
 SPARE = 8
+SERIES = [(k - 1) / math.factorial(k) for k in range(2, 12)]
 LIMIT = pltpu.CompilerParams(vmem_limit_bytes=16 * 1024 * 1024)
 FLIP = (((1,), (1,)), ((), ()))
 PLAIN = (((1,), (0,)), ((), ()))
@@ -26,6 +28,10 @@
     high = value.astype(BF16)
     low = (value - high.astype(F32)).astype(BF16)
     return (high, low)
+
+
+def times(p, q):
+    return (p[0] * q[0] - p[1] * q[1], p[0] * q[1] + p[1] * q[0])
 
 
 def dot(a, b, dims):
@@ -218,18 +224,15 @@
     t_re = t_re + near[:, 2 * poles : 3 * poles]
     t_im = t_im + near[:, 3 * poles :]
 
-    def times(p, q):
-        return (p[0] * q[0] - p[1] * q[1], p[0] * q[1] + p[1] * q[0])
-
     s, t = (s_re, s_im), (t_re, t_im)
     ct, lift = (line(2), line(3)), (line(4), line(5))
-    slope, ratio = (line(6), line(7)), (line(8), line(9))
+    slope, curve = (line(6), line(7)), (line(8), line(9))
     size, pole_re, w = line(10), line(11), (line(12), line(13))
     by_c = times(s, lift)
     first, second = times(s, slope), times(t, ct)
     by_w = (first[0] + second[0], first[1] + second[1])
-    third = times(s, ratio)
-    by_a = (size * by_w[0] - third[0], size * by_w[1] - third[1])
+    third = times(s, curve)
+    by_a = (size * second[0] + third[0], size * second[1] + third[1])
     by_dt = 2.0 * (by_w[0] * w[0] - by_w[1] * w[1])
     lane = lax.broadcasted_iota(jnp.int32, (1, poles), 1)
     by_skip = total(u_f * g_f)
@@ -288,25 +291,31 @@
             skip_ref[:, at : at + chips] = misc[2 + chan : 3 + chan]
 
 
+def lifted(w, growth, rise):
+    tail = (jnp.full_like(w[0], SERIES[-1]), jnp.zeros_like(w[0]))
+    for value in reversed(SERIES[:-1]):
+        tail = times(tail, w)
+        tail = (tail[0] + value, tail[1])
+    near = times(times(w, w), tail)
+    far = times(w, growth)
+    small = w[0] * w[0] + w[1] * w[1] < 0.25
+    return tuple(jnp.where(small, near[k], far[k] - rise[k]) for k in range(2))
+
+
 def pole_lines(step_size, pole_re, a_im, c_re, c_im):
-    w_re = step_size * pole_re
-    w_im = step_size * a_im
-    growth = jnp.exp(w_re)
-    cosine, sine = jnp.cos(w_im), jnp.sin(w_im)
-    half_sin = jnp.sin(0.5 * w_im)
-    e_re = jnp.expm1(w_re) * cosine - 2.0 * half_sin * half_sin
-    e_im = growth * sine
+    w = (step_size * pole_re, step_size * a_im)
+    growth = jnp.exp(w[0])
+    cosine, sine = jnp.cos(w[1]), jnp.sin(w[1])
+    half_sin = jnp.sin(0.5 * w[1])
+    rise = (jnp.expm1(w[0]) * cosine - 2.0 * half_sin * half_sin, growth * sine)
+    growth = (growth * cosine, growth * sine)
     modulus = pole_re * pole_re + a_im * a_im
-
-    def over_pole(re, im):
-        return ((re * pole_re + im * a_im) / modulus, (im * pole_re - re * a_im) / modulus)
-
-    ct_re, ct_im = over_pole(e_re * c_re - e_im * c_im, e_re * c_im + e_im * c_re)
-    lift = over_pole(e_re, e_im)
-    g_re, g_im = growth * cosine, growth * sine
-    slope = over_pole(g_re * c_re - g_im * c_im, g_re * c_im + g_im * c_re)
-    ratio = over_pole(ct_re, ct_im)
-    return (w_re, w_im, ct_re, ct_im) + lift + slope + ratio
+    inverse = (pole_re / modulus, -a_im / modulus)
+    c = (c_re, c_im)
+    lift = times(rise, inverse)
+    slope = times(times(growth, c), inverse)
+    curve = times(times(times(lifted(w, growth, rise), inverse), inverse), c)
+    return w + times(lift, c) + lift + slope + curve
 
 
 def vmem(count):

time: 59.1 us -> 59.1 us (level)
  no operation moved by 1% of the time
where the time goes in v5:
time: 59.1 us; the launch traced here: 58.9 us
  starting transfers between devices  19.3 us (33%)
  blocking collectives  17.5 us (30%)
  waiting for transfers between devices  11.2 us (19%)
  Pallas kernels  5.26 us (9%)
  local copies, waits for them, and re-layouts  2.83 us (5%)
  other arithmetic  1.87 us (3%)
  between operations  0.83 us (1%)
    all_to_all x1, blocking collectives, body(): lax.all_to_all(answer.reshape(chips, ROWS_OUT // 2, 2, span), CHIP, split...  17.5 us
    all_to_all x1, starting transfers between devices, body(): lax.all_to_all(sent.reshape(devices, ROWS_IN, span), OWNER, split_axis=0,...  15.7 us
    all_to_all x1, waiting for transfers between devices, body(): lax.all_to_all(sent.reshape(devices, ROWS_IN, span), OWNER, split_axis=0,...  9.99 us
    ppermute x1, starting transfers between devices, body(): other = lax.ppermute(mine, 'core', [(0, 1), (1, 0)])  3.64 us
    pallas_call x1, Pallas kernels, body(): pl.pallas_call(send_kernel, out_shape=jax.ShapeDtypeStruct((devices * ROW...  1.85 us
    pallas_call x1, Pallas kernels, body(): pl.pallas_call(functools.partial(core_kernel, batch), out_shape=jax.Shape...  1.49 us
    exp x1, other arithmetic, body(): step_size = jnp.exp(own_flat(log_dt))  1.37 us
    another operation x3, local copies, waits for them, and re-layouts, body(): jnp.stack([far * jnp.cos(w_im * span), far * jnp.sin(w_im * span)] + list...  1.35 us
  transfers between devices with their start and end apart: 2, of which 2 were waited for; matrix products, arithmetic and copies ran while one was open for 8% of the time, Pallas kernels for 1%

profile of v5, /device:TPU:1, one launch (start us, length us, event | category | flops | bytes accessed | tf_op | source)
XLA Modules:
  0.0 58.9 jit_solution(2427860599543572341)
XLA Ops:
  0.6 1.8 %shard_map.135 = bf16[1024,128]{1,0:T(8,128)(2,1)} custom-call(bf16[128,512]{1,0:T(8,128)(2,1)} %bitcast.102, bf16[128,512]{1,0:T(8,128)(2,1)} %bitcast.103), custom_call_target="tpu_custom_call" | custom-call | tf_op jit(solution)/shard_map/pallas_call | solution.py:334
  2.5 0.0 copy-start.4
  2.5 0.0 copy-start.5
  2.5 0.0 copy-start
  2.5 0.0 copy-start.1
  2.5 0.0 copy-start.3
  2.5 15.7 %all-to-all-start = ((bf16[256,4,128]{2,1,0:T(4,128)(2,1)}), bf16[256,4,128]{2,1,0:T(4,128)(2,1)S(1)}, u32[]{:S(2)}, u32[]{:S(2)}) async-start(bf16[256,4,128]{2,1,0:T(4,128)(2,1)} %bitcast.101), calls=%async_computation | async-start | bytes 524288 | tf_op jit(solution)/shard_map/all_to_all | solution.py:346
  18.2 0.0 copy-start.2
  18.2 0.0 copy-done.4
  18.3 0.0 copy-done.5
  18.3 0.6 %fusion.17 = (f32[1]{0:T(128)}, f32[1]{0:T(128)}, f32[1]{0:T(128)}, f32[1]{0:T(128)}) fusion(f32[512]{0:T(512)S(1)} %copy-done.4, s32[]{:T(128)S(6)} %select_n.46, s32[]{:T(128)S(6)} %select_n.45, f32[512]{0:T(512)S(1)} %copy-done.5), kind=kLoop, calls=%fused_computation.90 | loop fusion | bytes 40 | tf_op jit(solution)/shard_map/dynamic_slice | solution.py:368
  18.9 1.4 %maximum_exponential_fusion = f32[2]{0:T(128)S(1)} fusion(f32[1]{0:T(128)} %get-tuple-element.90, f32[1]{0:T(128)} %get-tuple-element.91), kind=kLoop, calls=%fused_computation.15 | loop fusion | flops 2 | bytes 16 | tf_op jit(solution)/shard_map/exp | solution.py:361
  20.2 0.1 broadcast_in_dim.12
  20.3 0.1 exp.224
  20.4 0.1 exp.221
  20.5 0.0 copy-done
  20.5 0.0 copy-done.1
  20.5 0.2 dynamic-slice_reduce_fusion.5
  20.7 0.0 copy-done.3
  20.7 0.0 copy-done.2
  20.7 0.2 dynamic-slice_reduce_fusion.1
  21.0 0.1 negate_bitcast_fusion
  21.1 0.1 fusion.16
  21.2 0.1 compare_select_fusion.1
  21.3 0.1 fusion.7
  21.4 0.1 multiply_subtract_fusion.4
  21.4 0.1 multiply_add_fusion.11
  21.5 0.1 copy.35.cols_ref
  21.6 0.8 %shard_map.136 = (bf16[512,256]{1,0:T(8,128)(2,1)S(1)}, bf16[512,256]{1,0:T(8,128)(2,1)S(1)}, bf16[512,256]{1,0:T(8,128)(2,1)S(1)}, bf16[512,256]{1,0:T(8,128)(2...) custom-call(f32[128,4]{1,0:T(8,128)S(1)} %copy.35.cols_ref), custom_call_target="tpu_custom_call" | custom-call | tf_op jit(solution)/shard_map/pallas_call | solution.py:381
  22.5 0.6 %stack_broadcast_in_dim.5 = f32[1,128]{1,0:T(1,128)S(1)} broadcast(f32[]{:T(128)} %bitcast.11), dimensions={} | broadcast | bytes 516 | tf_op jit(solution)/shard_map/stack;broadcast_in_dim | solution.py:371
  23.1 0.6 %stack_broadcast_in_dim.4 = f32[1,128]{1,0:T(1,128)S(1)} broadcast(f32[]{:T(128)} %bitcast.10), dimensions={} | broadcast | bytes 516 | tf_op jit(solution)/shard_map/stack;broadcast_in_dim | solution.py:371
  23.8 0.1 stack.5.prm_ref
  23.8 10.0 %all-to-all-done = bf16[256,4,128]{2,1,0:T(4,128)(2,1)S(1)} async-done(((bf16[256,4,128]{2,1,0:T(4,128)(2,1)}), bf16[256,4,128]{2,1,0:T(4,128)(2,1)S(1)}, u32[]{:S(2)}, u32[]{:S(2)}) %all-to-all-start) | async-done | bytes 262176 | tf_op jit(solution)/shard_map/all_to_all | solution.py:346
  33.8 1.5 %shard_map.137 = bf16[1280,128]{1,0:T(8,128)(2,1)S(1)} custom-call(bf16[1024,128]{1,0:T(8,128)(2,1)S(1)} %bitcast.100, bf16[512,256]{1,0:T(8,128)(2,1)S(1)} %get-tuple-element.23.fwd_hi, bf16[512,256]{1,0:T(8,128)(2,1)S(1)} %get-tuple-element.24.fwd_lo, bf16[512,256]{1,0:T(8,128)(2,1)S(1)} %get-tuple-element.25.rev_hi, ...), custom_call_target="tpu_custom_call" | custom-call | tf_op jit(solution)/shard_map/pallas_call | solution.py:389
  35.3 17.5 %all_to_all.10 = bf16[128,5,2,128]{3,2,1,0:T(2,128)(2,1)S(1)} all-to-all(bf16[128,5,2,128]{3,2,1,0:T(2,128)(2,1)S(1)} %bitcast.97), channel_id=1, replica_groups=mesh['dpair'=2,'core'=2,'ctx'=64] {'ctx','dpair'}, dimensions={0} | all-to-all | bytes 655360 | tf_op jit(solution)/shard_map/all_to_all | solution.py:400
  52.8 3.6 %collective-permute-start = (bf16[1280,128]{1,0:T(8,128)(2,1)S(1)}, bf16[1280,128]{1,0:T(8,128)(2,1)S(1)}, u32[]{:S(2)}, u32[]{:S(2)}) collective-permute-start(bf16[1280,128]{1,0:T(8,128)(2,1)S(1)} %bitcast.98), channel_id=1, source_target_pairs={{0,64},{64,0},{1,65},{65,1},{2,66},{66,2},{3,67},{67,3},{4,68},{68... | collective-permute-start | bytes 983048 | tf_op jit(solution)/shard_map/ppermute | solution.py:403
  56.5 1.3 %collective-permute-done.other_ref = bf16[1280,128]{1,0:T(8,128)(2,1)S(1)} collective-permute-done((bf16[1280,128]{1,0:T(8,128)(2,1)S(1)}, bf16[1280,128]{1,0:T(8,128)(2,1)S(1)}, u32[]{:S(2)}, u32[]{:S(2)}) %collective-permute-start) | collective-permute-done | bytes 327712 | tf_op jit(solution)/shard_map/ppermute | solution.py:403
  57.7 1.1 %shard_map.138 = (bf16[128,512]{1,0:T(8,128)(2,1)}, f32[64,512]{1,0:T(8,128)}, f32[64,512]{1,0:T(8,128)}, f32[64,512]{1,0:T(8,128)}, f32[64,512]{1,0:T(8,128)}, /*index=5*/f32[1,512]{1,0:T(1,128)}, f32[1,512]{1,0:T(1,128)}) custom-call(s32[1]{0:T(128)} %bitcast.core_ref, bf16[1280,128]{1,0:T(8,128)(2,1)S(1)} %bitcast.99, ...), custom_call_target="tpu_custom_call" | custom-call | tf_op jit(solution)/shard_map/pallas_call | solution.py:406
  (5 shorter events, 0.0 us)
Async XLA Ops:
  2.5 15.8 %copy-start.4 = (f32[512]{0:T(512)S(1)}, f32[512]{0:T(512)}, u32[]{:S(2)}) copy-start(f32[512]{0:T(512)} %param.15) | copy-start | bytes 6148
  2.5 15.8 %copy-start.5 = (f32[512]{0:T(512)S(1)}, f32[512]{0:T(512)}, u32[]{:S(2)}) copy-start(f32[512]{0:T(512)} %param.10) | copy-start | bytes 6148
  2.5 18.0 %copy-start = (f32[512,64]{0,1:T(8,128)S(1)}, f32[512,64]{0,1:T(8,128)}, u32[]{:S(2)}) copy-start(f32[512,64]{0,1:T(8,128)} %param.12) | copy-start | bytes 393220
  2.5 18.0 %copy-start.1 = (f32[512,64]{0,1:T(8,128)S(1)}, f32[512,64]{0,1:T(8,128)}, u32[]{:S(2)}) copy-start(f32[512,64]{0,1:T(8,128)} %param.11) | copy-start | bytes 393220
  2.5 18.2 %copy-start.3 = (f32[512,64]{0,1:T(8,128)S(1)}, f32[512,64]{0,1:T(8,128)}, u32[]{:S(2)}) copy-start(f32[512,64]{0,1:T(8,128)} %param.13) | copy-start | bytes 393220
  2.5 31.3 %all-to-all-start = ((bf16[256,4,128]{2,1,0:T(4,128)(2,1)}), bf16[256,4,128]{2,1,0:T(4,128)(2,1)S(1)}, u32[]{:S(2)}, u32[]{:S(2)}) async-start(bf16[256,4,128]{2,1,0:T(4,128)(2,1)} %bitcast.101), calls=%async_computation | async-start | bytes 524288 | tf_op jit(solution)/shard_map/all_to_all | solution.py:346
  18.2 2.5 %copy-start.2 = (f32[512,64]{0,1:T(8,128)S(1)}, f32[512,64]{0,1:T(8,128)}, u32[]{:S(2)}) copy-start(f32[512,64]{0,1:T(8,128)} %param.14) | copy-start | bytes 393220
  52.8 4.9 %collective-permute-start = (bf16[1280,128]{1,0:T(8,128)(2,1)S(1)}, bf16[1280,128]{1,0:T(8,128)(2,1)S(1)}, u32[]{:S(2)}, u32[]{:S(2)}) collective-permute-start(bf16[1280,128]{1,0:T(8,128)(2,1)S(1)} %bitcast.98), channel_id=1, source_target_pairs={{0,64},{64,0},{1,65},{65,1},{2,66},{66,2},{3,67},{67,3},{4,68},{68... | collective-permute-start | bytes 983048 | tf_op jit(solution)/shard_map/ppermute | solution.py:403

commit v6 on v5

--- a/solution.py
+++ b/solution.py
@@ -10,7 +10,6 @@
 from jax.sharding import PartitionSpec as P
 
 OWNER = ("ctx", "dpair", "core")
-CHIP = ("ctx", "dpair")
 F32 = jnp.float32
 BF16 = jnp.bfloat16
 ROWS_IN = 4
@@ -53,8 +52,11 @@
             for core in range(2):
                 at = half * owners + core * chips
                 piece = stage[part, :, at : at + chips].astype(F32).T
-                line = ROWS_IN * core + 2 * part + half
-                rows[pl.ds(line, chips, stride=2 * ROWS_IN), :] = piece
+                for pair in range(2):
+                    line = ROWS_IN * (2 * pair + core) + 2 * part + half
+                    rows[pl.ds(line, chips // 2, stride=4 * ROWS_IN), :] = piece[
+                        pair * chips // 2 : (pair + 1) * chips // 2
+                    ]
     pieces = sems.shape[0] - 2
     size = packed.shape[0] // pieces
     stores = []
@@ -268,12 +270,17 @@
     used = mine_ref.shape[0]
     chips = used // ROWS_OUT
     half = a_ref.shape[0]
-    core = core_ref[0]
-    rows[core, :used, :] = mine_ref[...].astype(F32)
-    rows[1 - core, :used, :] = other_ref[...].astype(F32)
+    core = core_ref[0] & 1
+    rows[0, :used, :] = mine_ref[...].astype(F32)
+    rows[1, :used, :] = other_ref[...].astype(F32)
+    odd = core ^ (core_ref[0] >> 1)
 
     def turned(owner, index):
-        return rows[owner, pl.ds(index, chips, stride=ROWS_OUT), :].T
+        halves = [
+            rows[odd ^ owner ^ pair, pl.ds(index + ROWS_OUT * pair, chips // 2, stride=2 * ROWS_OUT), :]
+            for pair in range(2)
+        ]
+        return jnp.concatenate(halves, axis=0).T
 
     for owner in range(2):
         for chan in range(2):
@@ -329,7 +336,7 @@
     poles = a_im.shape[1]
     assert channels == 2 * devices and span == 2 * poles
     chips = devices // 2
-    place = lax.axis_index("core") * chips + lax.axis_index(CHIP)
+    place = lax.axis_index("core") * chips + lax.axis_index(("dpair", "ctx"))
 
     sent = pl.pallas_call(
         send_kernel,
@@ -397,8 +404,14 @@
         + [pltpu.VMEM(((chips + SPARE) * ROWS_OUT, span), F32)],
         compiler_params=LIMIT,
     )(recv, *tables, prm)
+    groups = [[2 * chip + (first + chip) % 2 for chip in range(chips)] for first in range(2)]
     mine = lax.all_to_all(
-        answer.reshape(chips, ROWS_OUT // 2, 2, span), CHIP, split_axis=0, concat_axis=0, tiled=True
+        answer.reshape(chips, ROWS_OUT // 2, 2, span),
+        OWNER,
+        split_axis=0,
+        concat_axis=0,
+        tiled=True,
+        axis_index_groups=groups,
     ).reshape(chips * ROWS_OUT, span)
     other = lax.ppermute(mine, "core", [(0, 1), (1, 0)])
     line = jax.ShapeDtypeStruct((poles, channels), F32)
@@ -410,7 +423,7 @@
         out_specs=vmem(7),
         scratch_shapes=[pltpu.VMEM((2, (chips + SPARE) * ROWS_OUT, span), F32)],
         compiler_params=LIMIT,
-    )(lax.axis_index("core").reshape(1), mine, other)
+    )((lax.axis_index("core") + 2 * lax.axis_index("dpair")).reshape(1), mine, other)
     return (
         results[0][None],
         results[5].reshape(channels),

time: 59.1 us -> 58.7 us (level)
  starting transfers between devices: 19.3 us -> 15.7 us
  blocking collectives: 17.5 us -> 20.4 us
    ppermute x1, starting transfers between devices: 3.64 us -> 0.01 us  [body(): other = lax.ppermute(mine, 'core', [(0, 1), (1, 0)])]
    all_to_all x1, blocking collectives: 17.5 us -> 20.4 us  [body(): lax.all_to_all(answer.reshape(chips, ROWS_OUT // 2, 2, span), OWNER, spli...]
where the time goes in v6:
time: 58.7 us; the launch traced here: 58.5 us
  blocking collectives  20.4 us (35%)
  starting transfers between devices  15.7 us (27%)
  waiting for transfers between devices  11.6 us (20%)
  Pallas kernels  5.34 us (9%)
  local copies, waits for them, and re-layouts  2.83 us (5%)
  other arithmetic  1.87 us (3%)
  between operations  0.83 us (1%)
    all_to_all x1, blocking collectives, body(): lax.all_to_all(answer.reshape(chips, ROWS_OUT // 2, 2, span), OWNER, spli...  20.4 us
    all_to_all x1, starting transfers between devices, body(): lax.all_to_all(sent.reshape(devices, ROWS_IN, span), OWNER, split_axis=0,...  15.7 us
    all_to_all x1, waiting for transfers between devices, body(): lax.all_to_all(sent.reshape(devices, ROWS_IN, span), OWNER, split_axis=0,...  9.99 us
    pallas_call x1, Pallas kernels, body(): pl.pallas_call(send_kernel, out_shape=jax.ShapeDtypeStruct((devices * ROW...  1.92 us
    ppermute x1, waiting for transfers between devices, body(): other = lax.ppermute(mine, 'core', [(0, 1), (1, 0)])  1.63 us
    pallas_call x1, Pallas kernels, body(): pl.pallas_call(functools.partial(core_kernel, batch), out_shape=jax.Shape...  1.49 us
    exp x1, other arithmetic, body(): step_size = jnp.exp(own_flat(log_dt))  1.37 us
    another operation x3, local copies, waits for them, and re-layouts, body(): jnp.stack([far * jnp.cos(w_im * span), far * jnp.sin(w_im * span)] + list...  1.35 us
  transfers between devices with their start and end apart: 2, of which 2 were waited for; matrix products, arithmetic and copies ran while one was open for 8% of the time, Pallas kernels for 1%

profile of v6, /device:TPU:1, one launch (start us, length us, event | category | flops | bytes accessed | tf_op | source)
XLA Modules:
  0.0 58.5 jit_solution(67398205735648259)
XLA Ops:
  0.6 1.9 %shard_map.135 = bf16[1024,128]{1,0:T(8,128)(2,1)} custom-call(bf16[128,512]{1,0:T(8,128)(2,1)} %bitcast.102, bf16[128,512]{1,0:T(8,128)(2,1)} %bitcast.103), custom_call_target="tpu_custom_call" | custom-call | tf_op jit(solution)/shard_map/pallas_call | solution.py:341
  2.6 0.0 copy-start.4
  2.6 0.0 copy-start.5
  2.6 0.0 copy-start
  2.6 0.0 copy-start.1
  2.6 0.0 copy-start.3
  2.6 15.7 %all-to-all-start = ((bf16[256,4,128]{2,1,0:T(4,128)(2,1)}), bf16[256,4,128]{2,1,0:T(4,128)(2,1)S(1)}, u32[]{:S(2)}, u32[]{:S(2)}) async-start(bf16[256,4,128]{2,1,0:T(4,128)(2,1)} %bitcast.101), calls=%async_computation | async-start | bytes 524288 | tf_op jit(solution)/shard_map/all_to_all | solution.py:353
  18.3 0.0 copy-start.2
  18.3 0.0 copy-done.4
  18.3 0.0 copy-done.5
  18.3 0.6 %fusion.17 = (f32[1]{0:T(128)}, f32[1]{0:T(128)}, f32[1]{0:T(128)}, f32[1]{0:T(128)}) fusion(f32[512]{0:T(512)S(1)} %copy-done.4, s32[]{:T(128)S(6)} %select_n.46, s32[]{:T(128)S(6)} %select_n.45, f32[512]{0:T(512)S(1)} %copy-done.5), kind=kLoop, calls=%fused_computation.90 | loop fusion | bytes 40 | tf_op jit(solution)/shard_map/dynamic_slice | solution.py:375
  18.9 1.4 %maximum_exponential_fusion = f32[2]{0:T(128)S(1)} fusion(f32[1]{0:T(128)} %get-tuple-element.90, f32[1]{0:T(128)} %get-tuple-element.91), kind=kLoop, calls=%fused_computation.15 | loop fusion | flops 2 | bytes 16 | tf_op jit(solution)/shard_map/exp | solution.py:368
  20.3 0.1 broadcast_in_dim.12
  20.4 0.1 exp.224
  20.5 0.1 exp.221
  20.5 0.0 copy-done
  20.5 0.0 copy-done.1
  20.6 0.2 dynamic-slice_reduce_fusion.5
  20.8 0.0 copy-done.3
  20.8 0.0 copy-done.2
  20.8 0.2 dynamic-slice_reduce_fusion.1
  21.1 0.1 negate_bitcast_fusion
  21.1 0.1 fusion.16
  21.3 0.1 compare_select_fusion.1
  21.3 0.1 fusion.7
  21.4 0.1 multiply_subtract_fusion.4
  21.5 0.1 multiply_add_fusion.11
  21.6 0.1 copy.35.cols_ref
  21.7 0.8 %shard_map.136 = (bf16[512,256]{1,0:T(8,128)(2,1)S(1)}, bf16[512,256]{1,0:T(8,128)(2,1)S(1)}, bf16[512,256]{1,0:T(8,128)(2,1)S(1)}, bf16[512,256]{1,0:T(8,128)(2...) custom-call(f32[128,4]{1,0:T(8,128)S(1)} %copy.35.cols_ref), custom_call_target="tpu_custom_call" | custom-call | tf_op jit(solution)/shard_map/pallas_call | solution.py:388
  22.5 0.6 %stack_broadcast_in_dim.5 = f32[1,128]{1,0:T(1,128)S(1)} broadcast(f32[]{:T(128)} %bitcast.11), dimensions={} | broadcast | bytes 516 | tf_op jit(solution)/shard_map/stack;broadcast_in_dim | solution.py:378
  23.2 0.6 %stack_broadcast_in_dim.4 = f32[1,128]{1,0:T(1,128)S(1)} broadcast(f32[]{:T(128)} %bitcast.10), dimensions={} | broadcast | bytes 516 | tf_op jit(solution)/shard_map/stack;broadcast_in_dim | solution.py:378
  23.9 0.1 stack.5.prm_ref
  23.9 10.0 %all-to-all-done = bf16[256,4,128]{2,1,0:T(4,128)(2,1)S(1)} async-done(((bf16[256,4,128]{2,1,0:T(4,128)(2,1)}), bf16[256,4,128]{2,1,0:T(4,128)(2,1)S(1)}, u32[]{:S(2)}, u32[]{:S(2)}) %all-to-all-start) | async-done | bytes 262176 | tf_op jit(solution)/shard_map/all_to_all | solution.py:353
  33.9 1.5 %shard_map.137 = bf16[1280,128]{1,0:T(8,128)(2,1)S(1)} custom-call(bf16[1024,128]{1,0:T(8,128)(2,1)S(1)} %bitcast.100, bf16[512,256]{1,0:T(8,128)(2,1)S(1)} %get-tuple-element.23.fwd_hi, bf16[512,256]{1,0:T(8,128)(2,1)S(1)} %get-tuple-element.24.fwd_lo, bf16[512,256]{1,0:T(8,128)(2,1)S(1)} %get-tuple-element.25.rev_hi, ...), custom_call_target="tpu_custom_call" | custom-call | tf_op jit(solution)/shard_map/pallas_call | solution.py:396
  35.4 20.4 %all_to_all.10 = bf16[128,5,2,128]{3,2,1,0:T(2,128)(2,1)S(1)} all-to-all(bf16[128,5,2,128]{3,2,1,0:T(2,128)(2,1)S(1)} %bitcast.97), channel_id=1, replica_groups={{0,192,1,193,2,194,3,195,4,196,5,197,6,198,7,199,8,200,9,201,10,202,11,..., dimensions={0} | all-to-all | bytes 655360 | tf_op jit(solution)/shard_map/all_to_all | solution.py:408
  55.7 0.0 collective-permute-start
  55.8 1.6 %collective-permute-done.other_ref = bf16[1280,128]{1,0:T(8,128)(2,1)S(1)} collective-permute-done((bf16[1280,128]{1,0:T(8,128)(2,1)S(1)}, bf16[1280,128]{1,0:T(8,128)(2,1)S(1)}, u32[]{:S(2)}, u32[]{:S(2)}) %collective-permute-start) | collective-permute-done | bytes 327712 | tf_op jit(solution)/shard_map/ppermute | solution.py:416
  57.4 1.1 %shard_map.138 = (bf16[128,512]{1,0:T(8,128)(2,1)}, f32[64,512]{1,0:T(8,128)}, f32[64,512]{1,0:T(8,128)}, f32[64,512]{1,0:T(8,128)}, f32[64,512]{1,0:T(8,128)}, /*index=5*/f32[1,512]{1,0:T(1,128)}, f32[1,512]{1,0:T(1,128)}) custom-call(s32[1]{0:T(128)} %bitcast.core_ref, bf16[1280,128]{1,0:T(8,128)(2,1)S(1)} %bitcast.99, ...), custom_call_target="tpu_custom_call" | custom-call | tf_op jit(solution)/shard_map/pallas_call | solution.py:419
  (5 shorter events, 0.0 us)
Async XLA Ops:
  2.6 15.8 %copy-start.4 = (f32[512]{0:T(512)S(1)}, f32[512]{0:T(512)}, u32[]{:S(2)}) copy-start(f32[512]{0:T(512)} %param.15) | copy-start | bytes 6148
  2.6 15.8 %copy-start.5 = (f32[512]{0:T(512)S(1)}, f32[512]{0:T(512)}, u32[]{:S(2)}) copy-start(f32[512]{0:T(512)} %param.10) | copy-start | bytes 6148
  2.6 18.0 %copy-start = (f32[512,64]{0,1:T(8,128)S(1)}, f32[512,64]{0,1:T(8,128)}, u32[]{:S(2)}) copy-start(f32[512,64]{0,1:T(8,128)} %param.12) | copy-start | bytes 393220
  2.6 18.0 %copy-start.1 = (f32[512,64]{0,1:T(8,128)S(1)}, f32[512,64]{0,1:T(8,128)}, u32[]{:S(2)}) copy-start(f32[512,64]{0,1:T(8,128)} %param.11) | copy-start | bytes 393220
  2.6 18.2 %copy-start.3 = (f32[512,64]{0,1:T(8,128)S(1)}, f32[512,64]{0,1:T(8,128)}, u32[]{:S(2)}) copy-start(f32[512,64]{0,1:T(8,128)} %param.13) | copy-start | bytes 393220
  2.6 31.3 %all-to-all-start = ((bf16[256,4,128]{2,1,0:T(4,128)(2,1)}), bf16[256,4,128]{2,1,0:T(4,128)(2,1)S(1)}, u32[]{:S(2)}, u32[]{:S(2)}) async-start(bf16[256,4,128]{2,1,0:T(4,128)(2,1)} %bitcast.101), calls=%async_computation | async-start | bytes 524288 | tf_op jit(solution)/shard_map/all_to_all | solution.py:353
  18.3 2.5 %copy-start.2 = (f32[512,64]{0,1:T(8,128)S(1)}, f32[512,64]{0,1:T(8,128)}, u32[]{:S(2)}) copy-start(f32[512,64]{0,1:T(8,128)} %param.14) | copy-start | bytes 393220
  55.7 1.6 %collective-permute-start = (bf16[1280,128]{1,0:T(8,128)(2,1)S(1)}, bf16[1280,128]{1,0:T(8,128)(2,1)S(1)}, u32[]{:S(2)}, u32[]{:S(2)}) collective-permute-start(bf16[1280,128]{1,0:T(8,128)(2,1)S(1)} %bitcast.98), channel_id=1, source_target_pairs={{0,64},{64,0},{1,65},{65,1},{2,66},{66,2},{3,67},{67,3},{4,68},{68... | collective-permute-start | bytes 983048 | tf_op jit(solution)/shard_map/ppermute | solution.py:416

commit v7 on v6

--- a/solution.py
+++ b/solution.py
@@ -207,10 +207,10 @@
             t_re = t_re + (x * a - y * b) + (p * c - q * d)
             t_im = t_im + (x * b + y * a) + (p * d + q * c)
         if chunk > 0:
-            m = c + span * a
-            n = d + span * b
-            a, b = (e_re * a - e_im * b) + g_re[at, :], (e_re * b + e_im * a) + g_im[at, :]
-            c, d = (e_re * m - e_im * n) + d_re[at, :], (e_re * n + e_im * m) + d_im[at, :]
+            m, n = e_re * a - e_im * b, e_re * b + e_im * a
+            a, b = m + g_re[at, :], n + g_im[at, :]
+            m, n = span * m + d_re[at, :], span * n + d_im[at, :]
+            c, d = (e_re * c - e_im * d) + m, (e_re * d + e_im * c) + n
     s_re, s_im, t_re, t_im = total(s_re), total(s_im), total(t_re), total(t_im)
 
     state = jnp.concatenate([z_re[:sources, :], z_im[:sources, :]], axis=1)

time: 58.7 us -> 58.7 us (level)
  no operation moved by 1% of the time
where the time goes in v7:
time: 58.7 us; the launch traced here: 58.5 us
  blocking collectives  20.4 us (35%)
  starting transfers between devices  15.7 us (27%)
  waiting for transfers between devices  11.6 us (20%)
  Pallas kernels  5.35 us (9%)
  local copies, waits for them, and re-layouts  2.83 us (5%)
  other arithmetic  1.87 us (3%)
  between operations  0.83 us (1%)
    all_to_all x1, blocking collectives, body(): lax.all_to_all(answer.reshape(chips, ROWS_OUT // 2, 2, span), OWNER, spli...  20.4 us
    all_to_all x1, starting transfers between devices, body(): lax.all_to_all(sent.reshape(devices, ROWS_IN, span), OWNER, split_axis=0,...  15.7 us
    all_to_all x1, waiting for transfers between devices, body(): lax.all_to_all(sent.reshape(devices, ROWS_IN, span), OWNER, split_axis=0,...  9.99 us
    pallas_call x1, Pallas kernels, body(): pl.pallas_call(send_kernel, out_shape=jax.ShapeDtypeStruct((devices * ROW...  1.92 us
    ppermute x1, waiting for transfers between devices, body(): other = lax.ppermute(mine, 'core', [(0, 1), (1, 0)])  1.63 us
    pallas_call x1, Pallas kernels, body(): pl.pallas_call(functools.partial(core_kernel, batch), out_shape=jax.Shape...  1.5 us
    exp x1, other arithmetic, body(): step_size = jnp.exp(own_flat(log_dt))  1.37 us
    another operation x3, local copies, waits for them, and re-layouts, body(): jnp.stack([far * jnp.cos(w_im * span), far * jnp.sin(w_im * span)] + list...  1.35 us
  transfers between devices with their start and end apart: 2, of which 2 were waited for; matrix products, arithmetic and copies ran while one was open for 8% of the time, Pallas kernels for 1%

profile of v7, /device:TPU:1, one launch (start us, length us, event | category | flops | bytes accessed | tf_op | source)
XLA Modules:
  0.0 58.5 jit_solution(17970447877898306685)
XLA Ops:
  0.6 1.9 %shard_map.135 = bf16[1024,128]{1,0:T(8,128)(2,1)} custom-call(bf16[128,512]{1,0:T(8,128)(2,1)} %bitcast.102, bf16[128,512]{1,0:T(8,128)(2,1)} %bitcast.103), custom_call_target="tpu_custom_call" | custom-call | tf_op jit(solution)/shard_map/pallas_call | solution.py:341
  2.6 0.0 copy-start.4
  2.6 0.0 copy-start.5
  2.6 0.0 copy-start
  2.6 0.0 copy-start.1
  2.6 0.0 copy-start.3
  2.6 15.7 %all-to-all-start = ((bf16[256,4,128]{2,1,0:T(4,128)(2,1)}), bf16[256,4,128]{2,1,0:T(4,128)(2,1)S(1)}, u32[]{:S(2)}, u32[]{:S(2)}) async-start(bf16[256,4,128]{2,1,0:T(4,128)(2,1)} %bitcast.101), calls=%async_computation | async-start | bytes 524288 | tf_op jit(solution)/shard_map/all_to_all | solution.py:353
  18.3 0.0 copy-start.2
  18.3 0.0 copy-done.4
  18.3 0.0 copy-done.5
  18.3 0.6 %fusion.17 = (f32[1]{0:T(128)}, f32[1]{0:T(128)}, f32[1]{0:T(128)}, f32[1]{0:T(128)}) fusion(f32[512]{0:T(512)S(1)} %copy-done.4, s32[]{:T(128)S(6)} %select_n.46, s32[]{:T(128)S(6)} %select_n.45, f32[512]{0:T(512)S(1)} %copy-done.5), kind=kLoop, calls=%fused_computation.90 | loop fusion | bytes 40 | tf_op jit(solution)/shard_map/dynamic_slice | solution.py:375
  18.9 1.4 %maximum_exponential_fusion = f32[2]{0:T(128)S(1)} fusion(f32[1]{0:T(128)} %get-tuple-element.90, f32[1]{0:T(128)} %get-tuple-element.91), kind=kLoop, calls=%fused_computation.15 | loop fusion | flops 2 | bytes 16 | tf_op jit(solution)/shard_map/exp | solution.py:368
  20.3 0.1 broadcast_in_dim.12
  20.4 0.1 exp.224
  20.5 0.1 exp.221
  20.5 0.0 copy-done
  20.5 0.0 copy-done.1
  20.6 0.2 dynamic-slice_reduce_fusion.5
  20.8 0.0 copy-done.3
  20.8 0.0 copy-done.2
  20.8 0.2 dynamic-slice_reduce_fusion.1
  21.1 0.1 negate_bitcast_fusion
  21.1 0.1 fusion.16
  21.3 0.1 compare_select_fusion.1
  21.3 0.1 fusion.7
  21.4 0.1 multiply_subtract_fusion.4
  21.5 0.1 multiply_add_fusion.11
  21.6 0.1 copy.35.cols_ref
  21.7 0.8 %shard_map.136 = (bf16[512,256]{1,0:T(8,128)(2,1)S(1)}, bf16[512,256]{1,0:T(8,128)(2,1)S(1)}, bf16[512,256]{1,0:T(8,128)(2,1)S(1)}, bf16[512,256]{1,0:T(8,128)(2...) custom-call(f32[128,4]{1,0:T(8,128)S(1)} %copy.35.cols_ref), custom_call_target="tpu_custom_call" | custom-call | tf_op jit(solution)/shard_map/pallas_call | solution.py:388
  22.5 0.6 %stack_broadcast_in_dim.5 = f32[1,128]{1,0:T(1,128)S(1)} broadcast(f32[]{:T(128)} %bitcast.11), dimensions={} | broadcast | bytes 516 | tf_op jit(solution)/shard_map/stack;broadcast_in_dim | solution.py:378
  23.2 0.6 %stack_broadcast_in_dim.4 = f32[1,128]{1,0:T(1,128)S(1)} broadcast(f32[]{:T(128)} %bitcast.10), dimensions={} | broadcast | bytes 516 | tf_op jit(solution)/shard_map/stack;broadcast_in_dim | solution.py:378
  23.9 0.1 stack.5.prm_ref
  23.9 10.0 %all-to-all-done = bf16[256,4,128]{2,1,0:T(4,128)(2,1)S(1)} async-done(((bf16[256,4,128]{2,1,0:T(4,128)(2,1)}), bf16[256,4,128]{2,1,0:T(4,128)(2,1)S(1)}, u32[]{:S(2)}, u32[]{:S(2)}) %all-to-all-start) | async-done | bytes 262176 | tf_op jit(solution)/shard_map/all_to_all | solution.py:353
  33.9 1.5 %shard_map.137 = bf16[1280,128]{1,0:T(8,128)(2,1)S(1)} custom-call(bf16[1024,128]{1,0:T(8,128)(2,1)S(1)} %bitcast.100, bf16[512,256]{1,0:T(8,128)(2,1)S(1)} %get-tuple-element.23.fwd_hi, bf16[512,256]{1,0:T(8,128)(2,1)S(1)} %get-tuple-element.24.fwd_lo, bf16[512,256]{1,0:T(8,128)(2,1)S(1)} %get-tuple-element.25.rev_hi, ...), custom_call_target="tpu_custom_call" | custom-call | tf_op jit(solution)/shard_map/pallas_call | solution.py:396
  35.4 20.4 %all_to_all.10 = bf16[128,5,2,128]{3,2,1,0:T(2,128)(2,1)S(1)} all-to-all(bf16[128,5,2,128]{3,2,1,0:T(2,128)(2,1)S(1)} %bitcast.97), channel_id=1, replica_groups={{0,192,1,193,2,194,3,195,4,196,5,197,6,198,7,199,8,200,9,201,10,202,11,..., dimensions={0} | all-to-all | bytes 655360 | tf_op jit(solution)/shard_map/all_to_all | solution.py:408
  55.8 0.0 collective-permute-start
  55.8 1.6 %collective-permute-done.other_ref = bf16[1280,128]{1,0:T(8,128)(2,1)S(1)} collective-permute-done((bf16[1280,128]{1,0:T(8,128)(2,1)S(1)}, bf16[1280,128]{1,0:T(8,128)(2,1)S(1)}, u32[]{:S(2)}, u32[]{:S(2)}) %collective-permute-start) | collective-permute-done | bytes 327712 | tf_op jit(solution)/shard_map/ppermute | solution.py:416
  57.4 1.1 %shard_map.138 = (bf16[128,512]{1,0:T(8,128)(2,1)}, f32[64,512]{1,0:T(8,128)}, f32[64,512]{1,0:T(8,128)}, f32[64,512]{1,0:T(8,128)}, f32[64,512]{1,0:T(8,128)}, /*index=5*/f32[1,512]{1,0:T(1,128)}, f32[1,512]{1,0:T(1,128)}) custom-call(s32[1]{0:T(128)} %bitcast.core_ref, bf16[1280,128]{1,0:T(8,128)(2,1)S(1)} %bitcast.99, ...), custom_call_target="tpu_custom_call" | custom-call | tf_op jit(solution)/shard_map/pallas_call | solution.py:419
  (5 shorter events, 0.0 us)
Async XLA Ops:
  2.6 15.8 %copy-start.4 = (f32[512]{0:T(512)S(1)}, f32[512]{0:T(512)}, u32[]{:S(2)}) copy-start(f32[512]{0:T(512)} %param.15) | copy-start | bytes 6148
  2.6 15.8 %copy-start.5 = (f32[512]{0:T(512)S(1)}, f32[512]{0:T(512)}, u32[]{:S(2)}) copy-start(f32[512]{0:T(512)} %param.10) | copy-start | bytes 6148
  2.6 18.0 %copy-start = (f32[512,64]{0,1:T(8,128)S(1)}, f32[512,64]{0,1:T(8,128)}, u32[]{:S(2)}) copy-start(f32[512,64]{0,1:T(8,128)} %param.12) | copy-start | bytes 393220
  2.6 18.0 %copy-start.1 = (f32[512,64]{0,1:T(8,128)S(1)}, f32[512,64]{0,1:T(8,128)}, u32[]{:S(2)}) copy-start(f32[512,64]{0,1:T(8,128)} %param.11) | copy-start | bytes 393220
  2.6 18.2 %copy-start.3 = (f32[512,64]{0,1:T(8,128)S(1)}, f32[512,64]{0,1:T(8,128)}, u32[]{:S(2)}) copy-start(f32[512,64]{0,1:T(8,128)} %param.13) | copy-start | bytes 393220
  2.6 31.3 %all-to-all-start = ((bf16[256,4,128]{2,1,0:T(4,128)(2,1)}), bf16[256,4,128]{2,1,0:T(4,128)(2,1)S(1)}, u32[]{:S(2)}, u32[]{:S(2)}) async-start(bf16[256,4,128]{2,1,0:T(4,128)(2,1)} %bitcast.101), calls=%async_computation | async-start | bytes 524288 | tf_op jit(solution)/shard_map/all_to_all | solution.py:353
  18.3 2.5 %copy-start.2 = (f32[512,64]{0,1:T(8,128)S(1)}, f32[512,64]{0,1:T(8,128)}, u32[]{:S(2)}) copy-start(f32[512,64]{0,1:T(8,128)} %param.14) | copy-start | bytes 393220
  55.8 1.6 %collective-permute-start = (bf16[1280,128]{1,0:T(8,128)(2,1)S(1)}, bf16[1280,128]{1,0:T(8,128)(2,1)S(1)}, u32[]{:S(2)}, u32[]{:S(2)}) collective-permute-start(bf16[1280,128]{1,0:T(8,128)(2,1)S(1)} %bitcast.98), channel_id=1, source_target_pairs={{0,64},{64,0},{1,65},{65,1},{2,66},{66,2},{3,67},{67,3},{4,68},{68... | collective-permute-start | bytes 983048 | tf_op jit(solution)/shard_map/ppermute | solution.py:416
